TPU v7x, 256 devices: a whole 4x4x8 slice. The times are simulated.
256 devices in a mesh: seq: 32 (over z, x), tensor: 4 (over y), dp: 2 (over core).
Axes of the slice: x: 4, y: 4, z: 8, core: 2. Of those that a mesh axis runs over, the one named last changes fastest.
Arguments:
- queries: bfloat16 [32768, 4096], P(('dp', 'seq'), 'tensor'), parts along dimension 0, may hold values from -41 to 41
- database: bfloat16 [512, 128, 1024], P('seq'), may hold values from -36 to 36
- nbr_ids: int32 [512, 2], P(('dp', 'seq')), parts along dimension 0, may hold values from 0 to 511, as said below
- norm_gain: bfloat16 [1024], replicated, may hold values from 0.25 to 1.75
- enc_qkv: bfloat16 [3, 1024, 1024], P(None, None, 'tensor'), may hold values from -2.6 to 2.6
- enc_out: bfloat16 [1024, 1024], P('tensor'), may hold values from -0.75 to 0.75
- out_gain: bfloat16 [1024], replicated, may hold values from 0.25 to 1.75
- cca_kv: bfloat16 [2, 1024, 4096], P(None, None, 'tensor'), may hold values from -0.1875 to 0.1875
Outputs:
- attended: bfloat16 [32768, 4096], P(('dp', 'seq'), 'tensor'), parts along dimension 0
There are 2 independent parts, one for each index of `dp`. A program takes and returns all parts, laid end to end along the dimension named above; an argument that names none is the same for every part. Nothing has to cross between parts.
Inputs may be any that keep to these rules, and one draw needn't show every extreme that they name: `nbr_ids`: block id b lies in database shard b // 16, held by index b // 16 of seq. The 16 ids of one index of seq are distinct and at most 2 of them lie in one shard; in every draw one shard holds exactly 2 of the ids of every index of seq.
All inputs are finite; a program needn't handle non-finite values.
Results may differ from a plain program's by a relative error of at most 0.039.
Values may be sent and summed in bfloat16 or wider, within the bound.
A program may use at most 128 MiB of HBM per device.

v0:
```python
import math

import jax
import jax.numpy as jnp
from jax import lax
from jax.sharding import PartitionSpec as P

HDE = 64
HD = 128
M = 64


EPSILON = 1e-06


def shifted(block, axis, distance):
    devices = range(lax.axis_size(axis))
    route = [(i - distance, i) for i in devices if i - distance in devices]
    return lax.ppermute(block, axis, route)


def rms_scale(values, scale_gain):
    wide_values = values.astype(jnp.float32)
    mean_sq = jnp.mean(wide_values * wide_values, axis=-1, keepdims=True)
    return wide_values * lax.rsqrt(mean_sq + EPSILON) * scale_gain.astype(jnp.float32)


def head_mix(query_rows, key_rows, value_rows, head_size):
    leading, row_count, width_all = query_rows.shape
    key_count = key_rows.shape[1]
    head_count = width_all // head_size
    query_heads = query_rows.reshape(leading, row_count, head_count, head_size)
    key_heads = key_rows.reshape(leading, key_count, head_count, head_size)
    value_heads = value_rows.reshape(leading, key_count, head_count, head_size)
    scores = jnp.einsum(
        "aqhc,akhc->ahqk", query_heads, key_heads, preferred_element_type=jnp.float32
    ) / math.sqrt(head_size)
    attn_probs = jax.nn.softmax(scores, axis=-1).astype(jnp.bfloat16)
    mixed = jnp.einsum(
        "ahqk,akhc->aqhc", attn_probs, value_heads, preferred_element_type=jnp.float32
    )
    return mixed.astype(jnp.bfloat16).reshape(leading, row_count, width_all)


def with_prior(queries, pair_rows, prior_keys, prior_values):
    token_count, query_width = queries.shape
    edge_rows = M - 1
    window_count = pair_rows.shape[1]
    first_group = jnp.concatenate(
        [jnp.zeros((1, query_width), jnp.bfloat16), queries[:edge_rows]], 0
    )[None]
    later_groups = jnp.concatenate(
        [queries[edge_rows:], jnp.zeros((edge_rows, query_width), jnp.bfloat16)], 0
    )
    later_groups = later_groups.reshape(window_count, M, query_width)
    later_out = head_mix(later_groups, pair_rows[0], pair_rows[1], HD).reshape(
        token_count, query_width
    )
    first_out = head_mix(first_group, prior_keys, prior_values, HD)[0]
    return jnp.concatenate([first_out[1:], later_out[: token_count - edge_rows]], 0)


def per_device(queries, database, nbr_ids, norm_gain, enc_qkv, enc_out, out_gain, cca_kv):
    seq_count = lax.axis_size("seq")
    window_count, fanout = nbr_ids.shape
    block_count, neighbour_len, width_all = database.shape
    token_count, query_width = queries.shape
    request_list = nbr_ids.reshape(-1)
    request_count = request_list.shape[0]
    capacity = max(2, (request_count + seq_count - 1) // seq_count)
    owner_shard = request_list // block_count
    offset = request_list % block_count
    positions = jnp.arange(request_count, dtype=jnp.int32)
    earlier = (owner_shard[:, None] == owner_shard[None, :]) & (
        positions[None, :] < positions[:, None]
    )
    slot_rank = jnp.sum(earlier.astype(jnp.int32), axis=1)
    slot_index = owner_shard * capacity + slot_rank
    slot_ids = jnp.arange(seq_count * capacity, dtype=jnp.int32)
    slot_match = slot_ids[:, None] == slot_index[None, :]
    wanted = jnp.sum(jnp.where(slot_match, offset[None, :] + 1, 0), axis=1) - 1
    wanted = wanted.reshape(seq_count, capacity)
    safe_slots = jnp.maximum(
        lax.all_to_all(wanted, "seq", split_axis=0, concat_axis=0, tiled=True), 0
    )
    picked = jnp.take(database, safe_slots, axis=0)
    returned = lax.all_to_all(picked, "seq", split_axis=0, concat_axis=0, tiled=True)
    flat_slots = returned.reshape(seq_count * capacity, neighbour_len, returned.shape[-1])
    neighbours = jnp.take(flat_slots, slot_index, axis=0)
    normed = rms_scale(neighbours, norm_gain).astype(jnp.bfloat16)
    projected = jnp.einsum(
        "nrd,jde->jnre", normed, enc_qkv, preferred_element_type=jnp.float32
    ).astype(jnp.bfloat16)
    context = head_mix(projected[0], projected[1], projected[2], HDE)
    partial_sum = jnp.einsum("nrc,cd->nrd", context, enc_out, preferred_element_type=jnp.float32)
    summed = lax.psum(partial_sum.astype(jnp.bfloat16), "tensor").astype(jnp.float32)
    encoded = rms_scale(neighbours.astype(jnp.float32) + summed, out_gain).astype(jnp.bfloat16)
    pair_rows = jnp.einsum(
        "nrd,jde->jnre", encoded, cca_kv, preferred_element_type=jnp.float32
    ).astype(jnp.bfloat16)
    pair_rows = pair_rows.reshape(2, window_count, fanout * neighbour_len, query_width)
    prior_keys, prior_values = shifted(
        (pair_rows[0][window_count - 1 :], pair_rows[1][window_count - 1 :]), "seq", 1
    )
    attended = with_prior(queries, pair_rows, prior_keys, prior_values)
    return attended


def solution(mesh):
    placed = (
        P(("dp", "seq"), "tensor"),
        P("seq", None, None),
        P(("dp", "seq"), None),
        P(),
        P(None, None, "tensor"),
        P("tensor", None),
        P(),
        P(None, None, "tensor"),
    )
    return jax.shard_map(
        per_device,
        mesh=mesh,
        in_specs=placed,
        out_specs=P(("dp", "seq"), "tensor"),
        check_vma=False,
    )
```

profile of v0, /device:TPU:1, one launch (start us, length us, event | category | flops | bytes accessed | tf_op | source)
XLA Modules:
  0.0 654.9 jit_solution(4419269019572594286)
XLA Ops:
  6.5 0.0 copy-start
  6.5 0.9 copy.59
  7.4 0.1 reshape.284
  7.5 0.2 convert_reduce_fusion
  7.7 0.1 select_reduce_fusion
  7.8 0.1 sub.39
  7.9 20.2 %all_to_all.11 = s32[32,1,2]{2,1,0:T(1,128)S(1)} all-to-all(s32[32,1,2]{2,1,0:T(1,128)S(1)} %bitcast.113), channel_id=1, replica_groups=mesh['seq'=32,'tensor'=4,'dp'=2] {'seq'}, dimensions={0} | all-to-all | bytes 512 | tf_op jit(solution)/shard_map/all_to_all | solution.py:84
  28.2 0.1 maximum_reduce_fusion
  28.2 0.1 reshape.293
  28.4 0.1 copy.61
  28.5 0.1 copy.62
  28.6 9.7 %gather_fusion = bf16[64,128,1024]{2,1,0:T(8,128)(2,1)} fusion(bf16[16,128,1024]{2,1,0:T(8,128)(2,1)} %param.9, s32[1024]{0:T(1024)S(1)} %pad_clamp_fusion.1), kind=kCustom, calls=%fused_computation | custom fusion | bytes 33554688 | tf_op jit(solution)/shard_map/jit(_take)/gather | solution.py:86
  38.2 14.2 %broadcast_select_fusion = bf16[32,2,128,1024]{3,2,1,0:T(8,128)(2,1)} fusion(bf16[32,2,128,1024]{3,2,1,0:T(8,128)(2,1)} %bitcast.95, pred[32,2]{1,0:T(8,128)(4,1)S(1)} %copy.62), kind=kLoop, calls=%fused_computation.5 | loop fusion | flops 8388608 | bytes 33554496 | tf_op jit(solution)/shard_map/jit(_take)/select_n | solution.py:86
  52.5 5.3 all-to-all-start.1
  57.8 0.2 all-reduce.4.cloned.1.call-start
  58.0 0.1 reshape.286
  58.1 371.3 %all-to-all-done.1 = bf16[32,2,128,1024]{3,2,1,0:T(8,128)(2,1)} async-done(((bf16[32,2,128,1024]{3,2,1,0:T(8,128)(2,1)}), bf16[32,2,128,1024]{3,2,1,0:T(8,128)(2,1)}, u32[]{:S(2)}, u32[]{:S(2)}) %all-to-all-start.1) | async-done | bytes 16777248 | tf_op jit(solution)/shard_map/all_to_all | solution.py:87
  429.4 8.5 %gather_fusion.1 = bf16[16,128,1024]{2,1,0:T(8,128)(2,1)} fusion(bf16[64,128,1024]{2,1,0:T(8,128)(2,1)} %bitcast.3, s32[1024]{0:T(1024)S(1)} %pad_clamp_fusion), kind=kCustom, calls=%fused_computation.1 | custom fusion | bytes 8388672 | tf_op jit(solution)/shard_map/jit(_take)/gather | solution.py:89
  437.9 3.6 fusion.3
  441.5 3.9 convert_bitcast_fusion.1
  445.5 1.3 fusion.65
  446.8 2.3 copy.65
  449.0 1.3 copy.66
  450.3 0.7 copy.64
  451.0 5.1 fusion.66
  456.1 2.9 fusion.36
  459.1 0.0 copy-done.8
  459.1 0.0 copy-start.7
  459.1 3.2 convolution_convert_fusion
  462.3 0.0 all-reduce.4.cloned.1.call-update
  462.4 0.2 slice.59
  462.6 0.4 copy-done.10
  463.0 0.1 pad_bitcast_fusion
  463.2 0.3 copy.87
  463.5 124.7 %all-reduce.4.cloned.1.call-done = bf16[16,128,1024]{2,1,0:T(8,128)(2,1)} async-done(((bf16[16,128,1024]{2,1,0:T(8,128)(2,1)}), bf16[16,128,1024]{2,1,0:T(8,128)(2,1)}) %all-reduce.4.cloned.1.call-update) | async-done | bytes 4194320 | tf_op jit(solution)/shard_map/psum | solution.py:96
  588.1 5.4 multiply_reduce_fusion
  593.5 0.5 copy-done.5
  594.0 12.2 %convert_bitcast_fusion = bf16[2,16,128,1024]{3,2,0,1:T(8,128)(2,1)S(1)} fusion(bf16[16,128,1024]{2,1,0:T(8,128)(2,1)S(1)} %copy-done.5, bf16[2,1024,1024]{2,1,0:T(8,128)(2,1)} %param.15, f32[1024]{0:T(1024)S(1)} %convert_element_type.79, f32[16,128]{1,0:T(8,128)S(1)} %add_rsqrt_fusion, bf16[16,128,1024]{2,1,0:T(8,128)(2,1)S(1)} %copy-done.3, ...), kind=kOutput, calls=%fused_computation.12 | convolution fusion | flops 8608808960 | bytes 20983824 | tf_op jit(solution)/shard_map/nrd,jde->jnre/dot_general | solution.py:98
  606.2 0.1 fusion.63
  606.3 3.7 fusion.64
  610.0 1.1 copy.70
  611.1 3.1 collective-permute-start.1
  614.2 1.0 copy.69
  615.2 3.9 collective-permute-start
  619.1 3.3 copy.88
  622.4 1.6 fusion.14
  624.0 2.0 copy-done.6
  625.9 1.6 fusion.67
  627.5 0.6 copy-done.4
  628.1 3.0 copy.89
  631.1 11.9 %fusion.37 = bf16[8,64,8,128]{3,1,2,0:T(8,128)(2,1)S(1)} fusion(bf16[8,256,8,128]{3,2,1,0:T(8,128)(2,1)} %bitcast.100, f32[8,8,64]{2,1,0:T(8,128)S(1)} %fusion.67, f32[8,8,64,256]{3,2,1,0:T(8,128)} %copy-done.6), kind=kOutput, calls=%fused_computation.45 | convolution fusion | flops 274206976 | bytes 9453568 | tf_op jit(solution)/shard_map/ahqk,akhc->aqhc/dot_general | solution.py:39
  643.0 0.0 slice-start
  643.1 0.7 copy.78
  643.8 0.3 copy.107
  644.0 0.0 copy-start.1
  644.0 0.1 slice.74
  644.1 0.0 collective-permute-done.1
  644.1 0.2 convolution_multiply_fusion
  644.4 0.2 fusion.68
  644.6 0.0 collective-permute-done
  644.6 2.0 fusion.42
  646.6 0.1 slice.71
  646.7 0.1 copy.108
  646.8 1.2 pad_maximum_fusion
  (28 shorter events, 0.2 us)
Async XLA Ops:
  6.5 435.0 %copy-start = (bf16[3,1024,256]{2,1,0:T(8,128)(2,1)S(1)}, bf16[3,1024,256]{2,1,0:T(8,128)(2,1)}, u32[]{:S(2)}) copy-start(bf16[3,1024,256]{2,1,0:T(8,128)(2,1)} %param.12) | copy-start | bytes 4718596
  52.5 5.6 copy-start.9
  52.5 377.0 %all-to-all-start.1 = ((bf16[32,2,128,1024]{3,2,1,0:T(8,128)(2,1)}), bf16[32,2,128,1024]{3,2,1,0:T(8,128)(2,1)}, u32[]{:S(2)}, u32[]{:S(2)}) async-start(bf16[32,2,128,1024]{3,2,1,0:T(8,128)(2,1)} %broadcast_select_fusion), calls=%async_computation.1 | async-start | bytes 33554432 | tf_op jit(solution)/shard_map/all_to_all | solution.py:87
  57.8 530.3 %all-reduce.4.cloned.1.call-start = ((), (), s32[]{:S(2)}) async-start(), calls=%async_computation.2 | async-start | bytes 8388608 | tf_op jit(solution)/shard_map/psum | solution.py:96
  437.9 3.6 copy-start.2
  456.1 2.9 copy-start.8
  459.1 3.3 copy-start.7
  462.3 0.7 copy-start.10
  588.1 5.4 copy-start.3
  588.1 5.9 copy-start.5
  611.1 33.1 %collective-permute-start.1 = (bf16[1,256,1024]{1,2,0:T(8,128)(2,1)}, bf16[1,256,1024]{1,2,0:T(8,128)(2,1)S(1)}, u32[]{:S(2)}, u32[]{:S(2)}) collective-permute-start(bf16[1,256,1024]{1,2,0:T(8,128)(2,1)} %copy.70), channel_id=1, source_target_pairs={{0,8},{8,16},{16,24},{24,32},{32,40},{40,48},{48,56},{56,64},{64,7... | collective-permute-start | bytes 1572872 | tf_op jit(solution)/shard_map/ppermute | solution.py:19
  615.2 29.4 %collective-permute-start = (bf16[1,256,1024]{1,2,0:T(8,128)(2,1)}, bf16[1,256,1024]{1,2,0:T(8,128)(2,1)}, u32[]{:S(2)}, u32[]{:S(2)}) collective-permute-start(bf16[1,256,1024]{1,2,0:T(8,128)(2,1)} %copy.69), channel_id=1, source_target_pairs={{0,8},{8,16},{16,24},{24,32},{32,40},{40,48},{48,56},{56,64},{64,7... | collective-permute-start | bytes 1572872 | tf_op jit(solution)/shard_map/ppermute | solution.py:19
  623.9 2.0 copy-start.6
  625.9 2.2 copy-start.4
  643.0 1.1 slice-start
  644.0 4.0 copy-start.1
Sparse Core Ops, SparseCore 0:
  462.5 125.5 all-reduce.3
where the time goes:
time: 655 us
  waiting for transfers between devices  496 us (76%)
  matrix products  43.1 us (7%)
  local copies, waits for them, and re-layouts  42.6 us (7%)
  other arithmetic  26.6 us (4%)
  blocking collectives  20.2 us (3%)
  between operations  13.7 us (2%)
  starting transfers between devices  12.5 us (2%)
    all_to_all x1, waiting for transfers between devices, per_device(): lax.all_to_all(picked, 'seq', split_axis=0, concat_axis=0, tiled=True)  371 us
    psum x1, waiting for transfers between devices, per_device(): lax.psum(partial_sum.astype(jnp.bfloat16), 'tensor').astype(jnp.float32)  125 us
    all_to_all x1, blocking collectives, per_device(): lax.all_to_all(wanted, 'seq', split_axis=0, concat_axis=0, tiled=True)  20.2 us
    dot_general x3, matrix products, head_mix(): jnp.einsum('ahqk,akhc->aqhc', attn_probs, value_heads, preferred_element_...  16.8 us
    select_n x1, other arithmetic, per_device(): picked = jnp.take(database, safe_slots, axis=0)  14.2 us
  transfers between devices with their start and end apart: 4, of which 2 were waited for; matrix products, arithmetic and copies ran while one was open for 4% of the time, Pallas kernels for 0%

commit v1 on v0

v1 whole, which is shorter than its diff:
```python
import functools

import jax
import jax.numpy as jnp
from jax import lax
from jax.experimental import pallas as pl
from jax.experimental.pallas import tpu as pltpu
from jax.sharding import PartitionSpec as P

NZ, NX, NY, NC = 8, 4, 4, 2
BLOCKS = 16
ROWS = 128
PART = 16
D = 1024
SLOTS = 16
M = 64
EPS = 1e-6
CHUNKS = (256, 256, 256, 128, 128)
STARTS = tuple(sum(CHUNKS[:i]) for i in range(len(CHUNKS)))
NF = len(CHUNKS)
BF = jnp.bfloat16
F32 = jnp.float32


def body(
    ids_in, queries, database, norm_gain, enc_qkv, enc_out, out_gain, cca_kv,
    out,
    *scratch,
):
    scratch = list(scratch)

    def take(n):
        got = scratch[:n]
        del scratch[:n]
        return got

    pool, s1, r1, s2, r2, fin = (take(NF) for _ in range(6))
    (
        idv, ids_s, nb, wqkv, wout, wcca, enc, qraw, halo, qpad, back_out, back_in,
        normed, ctx, upd,
        id_sem, load_sem, z_send, z_recv, x_send, x_recv, a_send, a_recv, a_own,
        w_send, w_recv, b_send, b_recv, e_send, e_recv, h_send, h_recv,
    ) = scratch

    seq = lax.axis_index("seq")
    y = lax.axis_index("tensor")
    c = lax.axis_index("dp")
    z = seq // NX
    x = lax.rem(seq, NX)
    part = 2 * y + c

    def at(dz=0, dx=0, dy=0, dc=0):
        return {
            "seq": lax.rem(z + dz + NZ, NZ) * NX + lax.rem(x + dx + NX, NX),
            "tensor": lax.rem(y + dy + NY, NY),
            "dp": lax.rem(c + dc, NC),
        }

    def along(ds):
        return {"seq": lax.rem(seq + ds + NZ * NX, NZ * NX), "tensor": y, "dp": c}

    started = []

    def remote(src, dst, send_sem, recv_sem, device):
        return pltpu.make_async_remote_copy(
            src_ref=src, dst_ref=dst, send_sem=send_sem, recv_sem=recv_sem,
            device_id=device, device_id_type=pl.DeviceIdType.MESH,
        )

    def go(copy):
        copy.start()
        started.append(copy)

    def own_piece(f):
        return pltpu.make_async_copy(
            database.at[:, pl.ds(pl.multiple_of(PART * part, PART), PART), pl.ds(STARTS[f], CHUNKS[f])],
            pool[f].at[pl.ds(0, BLOCKS)], load_sem.at[f],
        )

    for f in range(NF):
        own_piece(f).start()
    ycol = pl.ds(pl.multiple_of(256 * y, 256), 256)
    local = [
        pltpu.make_async_copy(enc_qkv, wqkv.at[:, :, ycol], load_sem.at[NF]),
        pltpu.make_async_copy(enc_out, wout.at[ycol], load_sem.at[NF + 1]),
        pltpu.make_async_copy(cca_kv, wcca, load_sem.at[NF + 2]),
        pltpu.make_async_copy(queries, qraw, load_sem.at[NF + 3]),
    ]
    for copy in local:
        copy.start()
    idv[0] = jnp.zeros((8, 128), jnp.int32)
    idv[0, :, 0:2] = ids_in[...]

    greet = [at(dz=1), at(dz=-1), along(1), along(-1)]
    greet += [at(dx=dx, dc=dc) for dx in range(NX) for dc in range(NC) if dx or dc]
    greet += [at(dy=dy, dc=dc) for dy in range(1, NY) for dc in range(NC)]
    barrier = pltpu.get_barrier_semaphore()
    for device in greet:
        pl.semaphore_signal(barrier, inc=1, device_id=device, device_id_type=pl.DeviceIdType.MESH)
    pl.semaphore_wait(barrier, len(greet))

    def z_copy(f, right, k):
        count = BLOCKS if k < 4 else BLOCKS // 2
        shift = 0 if (k < 4 or right) else BLOCKS // 2
        source = (k - 1) if right else (NZ - (k - 1)) % NZ
        target = k if right else NZ - k
        i = (k - 1) if right else 4 + (k - 1)
        return remote(
            pool[f].at[pl.ds(BLOCKS * source + shift, count)],
            pool[f].at[pl.ds(BLOCKS * target + shift, count)],
            z_send.at[f, i], z_recv.at[f, i], at(dz=1 if right else -1),
        )

    def id_copy(dx, dc):
        slot = ((NX - dx) % NX) * 2 + dc
        return remote(idv.at[0], idv.at[slot], id_sem.at[slot], id_sem.at[8 + slot], at(dx=dx, dc=dc))

    def x_first(f, half):
        return remote(
            s1[f].at[half], r1[f].at[half], x_send.at[f, half], x_recv.at[f, half],
            at(dx=-1 if half == 0 else 1),
        )

    def x_second(f, right, half):
        i = 2 + 2 * right + half
        return remote(
            s2[f].at[right, half], r2[f].at[right, half], x_send.at[f, i], x_recv.at[f, i],
            at(dx=1 if right else -1),
        )

    def rows_of(f):
        return (slice(None), pl.ds(pl.multiple_of(PART * part, PART), PART), pl.ds(STARTS[f], CHUNKS[f]))

    def a_copy(f, dy, dc):
        t = lax.rem(y + dy, NY)
        i = dy * 2 + dc
        return remote(
            fin[f].at[dc, pl.ds(4 * t, 4)], nb.at[rows_of(f)],
            a_send.at[f, i], a_recv.at[f, i], at(dy=dy, dc=dc),
        )

    def a_local(f):
        return pltpu.make_async_copy(fin[f].at[0, pl.ds(4 * y, 4)], nb.at[rows_of(f)], a_own.at[f])

    def w_place(unit, rel, of=None):
        t = lax.rem(y + rel + NY, NY)
        if unit < 3:
            return wqkv.at[unit, pl.ds(pl.multiple_of(512 * c, 512), 512), pl.ds(pl.multiple_of(256 * t, 256), 256)]
        return wout.at[pl.ds(pl.multiple_of(256 * t + 128 * c, 128), 128)]

    def w_own(unit):
        if unit < 3:
            return enc_qkv.at[unit, pl.ds(pl.multiple_of(512 * c, 512), 512)]
        return enc_out.at[pl.ds(pl.multiple_of(128 * c, 128), 128)]

    def w_first(unit, right):
        i = unit + 4 * right
        return remote(w_own(unit), w_place(unit, 0), w_send.at[i], w_recv.at[i], at(dy=1 if right else -1))

    def w_second(unit):
        right = unit < 2
        return remote(
            w_place(unit, -1 if right else 1), w_place(unit, -1 if right else 1),
            w_send.at[8 + unit], w_recv.at[8 + unit], at(dy=1 if right else -1),
        )

    def w_twin(unit, rel):
        i = unit + 4 * (rel - 1)
        return remote(w_place(unit, rel), w_place(unit, rel), b_send.at[i], b_recv.at[i], at(dc=1))

    def e_place(late, n, rel):
        t = lax.rem(y + rel + NY, NY)
        return enc.at[2 * t + late, pl.ds(ROWS * n, ROWS)]

    def e_first(late, n, right):
        i = late * 6 + n * 2 + right
        return remote(
            e_place(late, n, 0), e_place(late, n, 0), e_send.at[i], e_recv.at[i], at(dy=1 if right else -1)
        )

    def e_second(late, n):
        i = late * 6 + 4 + n
        rel = -1 if n == 0 else 1
        return remote(
            e_place(late, n, rel), e_place(late, n, rel), e_send.at[i], e_recv.at[i], at(dy=-rel)
        )

    def h_query():
        return remote(queries.at[pl.ds(0, M)], halo, h_send.at[0], h_recv.at[0], along(-1))

    def h_back():
        return remote(back_out, back_in, h_send.at[1], h_recv.at[1], along(1))

    def select(f, requester, core, j, other):
        b = ids_s[2 * requester + core, j // 2, lax.rem(j, 2)]
        index = lax.rem(z - b // (NX * BLOCKS) + NZ, NZ) * BLOCKS + lax.rem(b, BLOCKS)
        owner = lax.rem(b // BLOCKS, NX)
        mine = pool[f][index]
        return mine if other is None else other(mine, owner)

    def first_select(f):
        def step(i, carry):
            core, j = i // 8, lax.rem(i, 8)
            s1[f][0, core, j] = select(f, 2, core, j, None)
            s1[f][1, core, j] = select(f, 2, core, 8 + j, None)
            return carry

        lax.fori_loop(0, 16, step, 0, unroll=2)

    def plain_select(f):
        def step(i, carry):
            core, j = i // 8, lax.rem(i, 8)
            s2[f][0, 1, core, j] = select(f, 3, core, 8 + j, None)
            s2[f][1, 0, core, j] = select(f, 1, core, j, None)
            return carry

        lax.fori_loop(0, 16, step, 0, unroll=2)

    def merge_select(f):
        def step(i, carry):
            core, j = i // 8, lax.rem(i, 8)
            s2[f][0, 0, core, j] = select(
                f, 3, core, j, lambda mine, owner: jnp.where(owner == x, mine, r1[f][0, core, j])
            )
            s2[f][1, 1, core, j] = select(
                f, 1, core, 8 + j, lambda mine, owner: jnp.where(owner == x, mine, r1[f][1, core, j])
            )
            return carry

        lax.fori_loop(0, 16, step, 0, unroll=2)

    def last_select(f):
        left, right = lax.rem(x + NX - 1, NX), lax.rem(x + 1, NX)

        def step(i, carry):
            core, j = i // 8, lax.rem(i, 8)

            def half0(mine, owner):
                far = jnp.where(owner == left, r2[f][1, 0, core, j], r2[f][0, 0, core, j])
                return jnp.where(owner == x, mine, far)

            def half1(mine, owner):
                far = jnp.where(owner == right, r2[f][0, 1, core, j], r2[f][1, 1, core, j])
                return jnp.where(owner == x, mine, far)

            fin[f][core, j] = select(f, 0, core, j, half0)
            fin[f][core, 8 + j] = select(f, 0, core, 8 + j, half1)
            return carry

        lax.fori_loop(0, 16, step, 0, unroll=2)

    def shift_queries():
        top = lax.broadcasted_iota(jnp.int32, (M, D), 0) == 0
        before = jnp.zeros((M, D), F32)
        for g in range(9):
            tile = qraw[pl.ds(M * g, M)] if g < 8 else halo[...]
            turned = pltpu.roll(tile.astype(F32), 1, 0)
            qpad[g] = jnp.where(top, before, turned).astype(BF)
            before = turned

    def encode(late):
        blocks = pl.ds(2 * late, 2)
        raw = nb[blocks].reshape(2 * ROWS, D).astype(F32)
        scale = lax.rsqrt(jnp.mean(raw * raw, axis=1, keepdims=True) + EPS)
        normed[...] = (raw * scale * norm_gain[...].astype(F32)).astype(BF)
        low = lax.broadcasted_iota(jnp.int32, (ROWS, 128), 1) < 64
        zero = jnp.zeros((ROWS, 128), BF)

        def heads(g, carry):
            cols = pl.ds(pl.multiple_of(256 * g, 256), 256)
            rows = normed[...]
            q, k, v = (
                jnp.dot(rows, wqkv[j, :, cols], preferred_element_type=F32).astype(BF) for j in range(3)
            )
            mixed = []
            for n in range(2):
                pairs = []
                for p in range(2):
                    cut = (slice(ROWS * n, ROWS * (n + 1)), slice(128 * p, 128 * (p + 1)))
                    qp, kp, vp = q[cut], k[cut], v[cut]
                    k2 = jnp.concatenate([jnp.where(low, kp, zero), jnp.where(low, zero, kp)], axis=0)
                    v2 = jnp.concatenate([jnp.where(low, vp, zero), jnp.where(low, zero, vp)], axis=0)
                    s = lax.dot_general(qp, k2, (((1,), (1,)), ((), ())), preferred_element_type=F32) * 0.125
                    probs = []
                    for h in range(2):
                        sh = s[:, 128 * h : 128 * (h + 1)]
                        e = jnp.exp(sh - jnp.max(sh, axis=1, keepdims=True))
                        probs.append((e / jnp.sum(e, axis=1, keepdims=True)).astype(BF))
                    pairs.append(jnp.dot(jnp.concatenate(probs, axis=1), v2, preferred_element_type=F32).astype(BF))
                mixed.append(jnp.concatenate(pairs, axis=1))
            ctx[:, cols] = jnp.concatenate(mixed, axis=0)
            return carry

        lax.fori_loop(0, 4, heads, 0)

        def project(g, carry):
            cols = pl.ds(pl.multiple_of(256 * g, 256), 256)
            upd[:, cols] = jnp.dot(ctx[...], wout[:, cols], preferred_element_type=F32)
            return carry

        lax.fori_loop(0, 4, project, 0)
        total = upd[...] + nb[blocks].reshape(2 * ROWS, D).astype(F32)
        scale = lax.rsqrt(jnp.mean(total * total, axis=1, keepdims=True) + EPS)
        enc[2 * y + late] = (total * scale * out_gain[...].astype(F32)).astype(BF)

    def attend(rel, late):
        w = 2 * lax.rem(y + rel + NY, NY) + late

        def heads(g, carry):
            cols = pl.ds(pl.multiple_of(256 * g, 256), 256)
            rows = enc[w]
            k = jnp.dot(rows, wcca[0, :, cols], preferred_element_type=F32).astype(BF)
            v = jnp.dot(rows, wcca[1, :, cols], preferred_element_type=F32).astype(BF)
            q = qpad[w + 1, :, cols]
            mixed = []
            for h in range(2):
                cut = slice(128 * h, 128 * (h + 1))
                s = lax.dot_general(
                    q[:, cut], k[:, cut], (((1,), (1,)), ((), ())), preferred_element_type=F32
                ) * (128.0 ** -0.5)
                e = jnp.exp(s - jnp.max(s, axis=1, keepdims=True))
                p = (e / jnp.sum(e, axis=1, keepdims=True)).astype(BF)
                mixed.append(jnp.dot(p, v[:, cut], preferred_element_type=F32).astype(BF))
            out[w + 1, :, cols] = jnp.concatenate(mixed, axis=1)
            return carry

        lax.fori_loop(0, 4, heads, 0)

    def z_step(f, k):
        if k == 1:
            own_piece(f).wait()
        else:
            z_copy(f, True, k - 1).wait_recv()
            z_copy(f, False, k - 1).wait_recv()
        go(z_copy(f, True, k))
        go(z_copy(f, False, k))

    def x_step1(f):
        z_copy(f, True, 4).wait_recv()
        z_copy(f, False, 4).wait_recv()
        first_select(f)
        go(x_first(f, 0))
        go(x_first(f, 1))
        plain_select(f)
        go(x_second(f, 0, 1))
        go(x_second(f, 1, 0))

    def x_step2(f):
        x_first(f, 0).wait_recv()
        x_first(f, 1).wait_recv()
        merge_select(f)
        go(x_second(f, 0, 0))
        go(x_second(f, 1, 1))

    others = [(dy, dc) for dy in (2, 1, 3, 0) for dc in range(NC) if dy or dc]

    def x_step3(f):
        for right in range(2):
            for half in range(2):
                x_second(f, right, half).wait_recv()
        last_select(f)
        for dy, dc in others:
            go(a_copy(f, dy, dc))
        a_local(f).start()

    def w_forward(pos):
        for right in (1, 0):
            unit = pos if right else (pos + 2) % 4
            w_first(unit, right).wait_recv()
            if pos < 2:
                go(w_second(unit))
            go(w_twin(unit, 3 if right else 1))

    for f in range(2):
        z_step(f, 1)
    for dx in range(NX):
        for dc in range(NC):
            if dx or dc:
                go(id_copy(dx, dc))
    go(h_query())
    for pos in range(4):
        go(w_first(pos, 1))
        go(w_first((pos + 2) % 4, 0))

    events = []
    for f in range(NF):
        for k in range(1, 5):
            if k > 1 or f > 1:
                events.append((2 * f + k, 0, functools.partial(z_step, f, k)))
        events.append((2 * f + 5, 2, functools.partial(x_step1, f)))
        events.append((2 * f + 6, 3, functools.partial(x_step2, f)))
        events.append((2 * f + 7, 4, functools.partial(x_step3, f)))

    def ids_ready():
        for dx in range(NX):
            for dc in range(NC):
                if dx or dc:
                    id_copy(dx, dc).wait_recv()
        copy = pltpu.make_async_copy(idv, ids_s, id_sem.at[0])
        copy.start()
        copy.wait()

    def queries_ready():
        local[3].wait()
        h_query().wait_recv()
        shift_queries()

    events.append((3, 1, ids_ready))
    events.append((4, 1, queries_ready))
    for pos, tick in enumerate((4, 6, 8, 10)):
        events.append((tick, 5, functools.partial(w_forward, pos)))
    events.sort(key=lambda e: e[:2])
    for _, _, event in events:
        event()

    for unit in range(4):
        w_second(unit).wait_recv()
        go(w_twin(unit, 2))
    for f in range(NF):
        for dy, dc in others:
            a_copy(f, dy, dc).wait_recv()
        a_local(f).wait()
    for rel in range(1, 4):
        for unit in range(4):
            w_twin(unit, rel).wait_recv()
    for i in range(3):
        local[i].wait()

    def e_forward(late):
        for n in range(2):
            rel_right = n == 0
            e_first(late, n, 1 if rel_right else 0).wait_recv()
            go(e_second(late, n))

    for late in (1, 0):
        encode(late)
        go(e_first(late, 0, 1))
        go(e_first(late, 1, 0))
        go(e_first(late, 1, 1))
        go(e_first(late, 0, 0))
    e_forward(1)
    attend(0, 1)
    attend(0, 0)
    e_first(1, 1, 1).wait_recv()
    attend(-1, 1)
    e_first(1, 0, 0).wait_recv()
    attend(1, 1)
    e_forward(0)
    e_first(0, 1, 1).wait_recv()
    attend(-1, 0)
    e_first(0, 0, 0).wait_recv()
    attend(1, 0)
    for n in range(2):
        e_second(1, n).wait_recv()
    attend(2, 1)
    back_out[...] = out[8]
    go(h_back())
    for n in range(2):
        e_second(0, n).wait_recv()
    attend(2, 0)
    h_back().wait_recv()
    out[0] = back_in[...]
    for copy in started:
        copy.wait_send()


def fused(ids, queries, database, norm_gain, enc_qkv, enc_out, out_gain, cca_kv):
    dma = pltpu.SemaphoreType.DMA
    per_chunk = lambda *lead: [pltpu.VMEM(lead + (PART, w), BF) for w in CHUNKS]
    scratch = (
        per_chunk(NZ * BLOCKS)
        + per_chunk(2, 2, 8) + per_chunk(2, 2, 8)
        + per_chunk(2, 2, 2, 8) + per_chunk(2, 2, 2, 8)
        + per_chunk(2, SLOTS)
    )
    scratch += [
        pltpu.VMEM((8, 8, 128), jnp.int32),
        pltpu.SMEM((8, 8, 128), jnp.int32),
        pltpu.VMEM((4, ROWS, D), BF),
        pltpu.VMEM((3, D, D), BF),
        pltpu.VMEM((D, D), BF),
        pltpu.VMEM((2, D, D), BF),
        pltpu.VMEM((8, 2 * ROWS, D), BF),
        pltpu.VMEM((8 * M, D), BF),
        pltpu.VMEM((M, D), BF),
        pltpu.VMEM((9, M, D), BF),
        pltpu.VMEM((M, D), BF),
        pltpu.VMEM((M, D), BF),
        pltpu.VMEM((2 * ROWS, D), BF),
        pltpu.VMEM((2 * ROWS, D), BF),
        pltpu.VMEM((2 * ROWS, D), F32),
        dma((16,)), dma((NF + 4,)), dma((NF, 8)), dma((NF, 8)), dma((NF, 6)), dma((NF, 6)),
        dma((NF, 8)), dma((NF, 8)), dma((NF,)),
        dma((12,)), dma((12,)), dma((12,)), dma((12,)), dma((12,)), dma((12,)), dma((2,)), dma((2,)),
    ]
    vmem = pl.BlockSpec(memory_space=pltpu.VMEM)
    hbm = pl.BlockSpec(memory_space=pl.ANY)
    return pl.pallas_call(
        body,
        out_shape=jax.ShapeDtypeStruct((9, M, D), BF),
        in_specs=[vmem, hbm, hbm, vmem, hbm, hbm, vmem, hbm],
        out_specs=vmem,
        scratch_shapes=scratch,
        compiler_params=pltpu.CompilerParams(
            collective_id=0, has_side_effects=True, vmem_limit_bytes=56 * 2**20
        ),
        cost_estimate=pl.CostEstimate(flops=14 * 10**9, bytes_accessed=12 * 2**20, transcendentals=4 * 10**6),
    )(ids, queries, database, norm_gain, enc_qkv, enc_out, out_gain, cca_kv)


def per_device(queries, database, nbr_ids, norm_gain, enc_qkv, enc_out, out_gain, cca_kv):
    groups = fused(
        nbr_ids, queries, database, norm_gain.reshape(1, D), enc_qkv, enc_out, out_gain.reshape(1, D), cca_kv
    )
    tokens = queries.shape[0]
    attended = groups.reshape(9 * M, D)[1 : tokens + 1]
    unserved = (lax.axis_index("seq") == 0) & (lax.broadcasted_iota(jnp.int32, (tokens, 1), 0) < M - 1)
    return jnp.where(unserved, jnp.zeros((), BF), attended)


def solution(mesh):
    placed = (
        P(("dp", "seq"), "tensor"),
        P("seq", None, None),
        P(("dp", "seq"), None),
        P(),
        P(None, None, "tensor"),
        P("tensor", None),
        P(),
        P(None, None, "tensor"),
    )
    return jax.shard_map(
        per_device,
        mesh=mesh,
        in_specs=placed,
        out_specs=P(("dp", "seq"), "tensor"),
        check_vma=False,
    )
```

time: 655 us -> 149 us (0.23)
  waiting for transfers between devices: 496 us -> 0 us
  Pallas kernels: 0 us -> 142 us
  matrix products: 43.1 us -> 0 us
  local copies, waits for them, and re-layouts: 42.6 us -> 3.89 us
  other arithmetic: 26.6 us -> 2.52 us
  blocking collectives: 20.2 us -> 0 us
  between operations: 13.7 us -> 0.01 us
  starting transfers between devices: 12.5 us -> 0 us
    all_to_all x1 -> x0, waiting for transfers between devices: 371 us -> none  [per_device(): lax.all_to_all(picked, 'seq', split_axis=0, concat_axis=0, tiled=True)]
    pallas_call x0 -> x1, Pallas kernels: none -> 142 us  [fused(): pl.pallas_call(body, out_shape=jax.ShapeDtypeStruct((9, M, D), BF), in_sp...]
    psum x1 -> x0, waiting for transfers between devices: 125 us -> none  [per_device(): lax.psum(partial_sum.astype(jnp.bfloat16), 'tensor').astype(jnp.float32)]
    dot_general x8 -> x0, matrix products: 38 us -> none  [the longest x3 16.8 us: head_mix(): jnp.einsum('ahqk,akhc->aqhc', attn_probs, value_heads, preferred_element_...]
    all_to_all x1 -> x0, blocking collectives: 20.2 us -> none  [per_device(): lax.all_to_all(wanted, 'seq', split_axis=0, concat_axis=0, tiled=True)]
    gather x2 -> x0, local copies, waits for them, and re-layouts: 18.2 us -> none  [the longest x1 9.66 us: per_device(): picked = jnp.take(database, safe_slots, axis=0)]
    slice x14 -> x0, local copies, waits for them, and re-layouts: 11.8 us -> none  [the longest x4 5.51 us: per_device(): context = head_mix(projected[0], projected[1], projected[2], HDE)]
    select_n x3 -> x1, other arithmetic: 14.2 us -> 2.52 us  [per_device(): return jnp.where(unserved, jnp.zeros((), BF), attended)]
  transfers between devices with their start and end apart: 4 -> 0, of which waited for: 2 -> 0; matrix products, arithmetic and copies ran while one was open for 4% -> 0% of each run, Pallas kernels for 0% -> 0%
where the time goes in v1:
time: 149 us
  Pallas kernels  142 us (95%)
  local copies, waits for them, and re-layouts  3.89 us (3%)
  other arithmetic  2.52 us (2%)
    pallas_call x1, Pallas kernels, fused(): pl.pallas_call(body, out_shape=jax.ShapeDtypeStruct((9, M, D), BF), in_sp...  142 us

profile of v1, /device:TPU:1, one launch (start us, length us, event | category | flops | bytes accessed | tf_op | source)
XLA Modules:
  0.0 148.9 jit_solution(3249549663514910205)
XLA Ops:
  0.0 1.3 copy.9.ids_in
  1.4 1.3 reshape.16.norm_gain
  2.6 1.3 reshape.17.out_gain
  3.9 142.4 %shard_map.82 = bf16[9,64,1024]{2,1,0:T(8,128)(2,1)} custom-call(s32[8,2]{1,0:T(8,128)} %copy.9.ids_in, bf16[512,1024]{1,0:T(8,128)(2,1)} %queries.1, bf16[16,128,1024]{2,1,0:T(8,128)(2,1)} %database.1, bf16[1,1024]{1,0:T(2,128)(2,1)} %reshape.16.norm_gain, bf16[3,1024,256]{2,1,0:T(8,128)(2,1)} %enc_qkv.1, bf16[256,1024]{1,0:T(8,128)(2,1)} %enc_out.1, ...), custom_call_target="tpu_custom_call" | custom-call | flops 14000000000 | bytes 12582912 | tf_op jit(solution)/shard_map/pallas_call | solution.py:498
  146.3 2.5 %slice_select_fusion = bf16[512,1024]{1,0:T(8,128)(2,1)} fusion(bf16[576,1024]{1,0:T(8,128)(2,1)} %bitcast.1, pred[512]{0:T(512)(128)(4,1)S(1)} %fusion), kind=kLoop, calls=%fused_computation | loop fusion | flops 524288 | bytes 2097664 | tf_op jit(solution)/shard_map/jit(_where)/select_n | solution.py:518
  (1 shorter events, 0.0 us)

commit v2 on v1

v2 whole, which is shorter than its diff:
```python
import functools

import jax
import jax.numpy as jnp
from jax import lax
from jax.experimental import pallas as pl
from jax.experimental.pallas import tpu as pltpu
from jax.sharding import PartitionSpec as P

NZ, NX, NY, NC = 8, 4, 4, 2
BLOCKS = 16
ROWS = 128
PART = 16
D = 1024
SLOTS = 16
M = 64
EPS = 1e-6
NF = 8
WIDE = D // NF
UNITS = ((1, (0, 1)), (1, (2, 3)), (1, (4, 5)), (1, (6,)), (1, (7,)), (0, (0, 1, 2, 3)), (0, (4, 5, 6, 7)))
DIRECT = ()
SHARED = 12
EACH = SHARED // NY
PLACES = tuple(3 * t + (m if t % 2 == 0 else 2 - m) for t in range(NY) for m in range(EACH)) + (12, 13, 14, 15)
ORDER = (
    ('z', 2, 1), ('z', 0, 1), ('z', 1, 1), ('z', 3, 1), ('z', 0, 2), ('w0', 0),
    ('z', 1, 2), ('z', 2, 2), ('z', 3, 2), ('w0', 1), ('z', 0, 3), ('z', 1, 3),
    ('w0', 2), ('z', 3, 3), ('ids',), ('z', 0, 4), ('z', 2, 3), ('z', 1, 4),
    ('z', 4, 1), ('zd', 0), ('z', 7, 1), ('z', 2, 4), ('z', 3, 4), ('z', 5, 1),
    ('zd', 1), ('x1', 0), ('z', 4, 2), ('wf', 0), ('z', 7, 2), ('zd', 2),
    ('zd', 3), ('x1', 1), ('z', 6, 1), ('x2', 0), ('z', 5, 2), ('wf', 1),
    ('z', 7, 3), ('x1', 5), ('z', 4, 3), ('z', 5, 3), ('x2', 1), ('z', 7, 4),
    ('w0', 3), ('z', 6, 2), ('x3', 0), ('z', 4, 4), ('x2', 5), ('z', 5, 4),
    ('wr', 0), ('zd', 7), ('x1', 4), ('z', 6, 3), ('zd', 4), ('zd', 5),
    ('x1', 2), ('wr', 1), ('z', 6, 4), ('x3', 1), ('x2', 4), ('x2', 2),
    ('zd', 6), ('x1', 3), ('wf', 2), ('x3', 5), ('x1', 6), ('q',),
    ('x2', 3), ('x3', 2), ('x2', 6), ('x3', 4), ('wf', 3), ('x3', 3),
    ('x3', 6), ('en', 0), ('en', 1), ('en', 2), ('en', 3), ('er', 0, 0),
    ('er', 0, 1), ('er', 0, 2), ('ef', 0), ('er', 1, 0), ('er', 1, 1), ('er', 1, 2),
    ('at', 6), ('ef', 1), ('at', 7), ('hb',), ('at', 0), ('ar',),
    ('at', 1), ('ef', 2), ('at', 2), ('at', 3), ('at', 4), ('at', 5),
)
LOG2E = 1.4426950408889634
BF = jnp.bfloat16
F32 = jnp.float32


def body(
    ids_in, queries, database, norm_gain, enc_qkv, enc_out, out_gain, cca_kv,
    out,
    *scratch,
):
    scratch = list(scratch)

    def take(n):
        got = scratch[:n]
        del scratch[:n]
        return got

    pool = take(NF)
    s1, r1, s2, r2, fin = (take(len(UNITS)) for _ in range(5))
    (
        idv, ids_s, table, nbp, nbr, wqkv, wout, wcca, enc, qraw, halo, qpad, back_out, back_in,
        normed, ctx, upd, qs, kv,
        id_sem, load_sem, z_send, z_recv, x_send, x_recv, a_send, a_recv, a_own,
        w_send, w_recv, b_send, b_recv, e_send, e_recv, h_send, h_recv,
    ) = scratch

    seq = lax.axis_index("seq")
    y = lax.axis_index("tensor")
    c = lax.axis_index("dp")
    z = seq // NX
    x = lax.rem(seq, NX)
    part = 2 * y + c

    def at(dz=0, dx=0, dy=0, dc=0):
        return {
            "seq": lax.rem(z + dz + NZ, NZ) * NX + lax.rem(x + dx + NX, NX),
            "tensor": lax.rem(y + dy + NY, NY),
            "dp": lax.rem(c + dc, NC),
        }

    def along(ds):
        return {"seq": lax.rem(seq + ds + NZ * NX, NZ * NX), "tensor": y, "dp": c}

    started = []

    def remote(src, dst, send_sem, recv_sem, device):
        return pltpu.make_async_remote_copy(
            src_ref=src, dst_ref=dst, send_sem=send_sem, recv_sem=recv_sem,
            device_id=device, device_id_type=pl.DeviceIdType.MESH,
        )

    def go(copy):
        copy.start()
        started.append(copy)

    def own_piece(f):
        return pltpu.make_async_copy(
            database.at[:, pl.ds(pl.multiple_of(PART * part, PART), PART), pl.ds(WIDE * f, WIDE)],
            pool[f].at[pl.ds(0, BLOCKS)], load_sem.at[f],
        )

    for f in range(NF):
        own_piece(f).start()
    ycol = pl.ds(pl.multiple_of(256 * y, 256), 256)
    local = [
        pltpu.make_async_copy(enc_qkv, wqkv.at[:, :, ycol], load_sem.at[NF]),
        pltpu.make_async_copy(enc_out, wout.at[ycol], load_sem.at[NF + 1]),
        pltpu.make_async_copy(cca_kv, wcca, load_sem.at[NF + 2]),
        pltpu.make_async_copy(queries, qraw, load_sem.at[NF + 3]),
    ]
    for copy in local:
        copy.start()
    idv[0] = jnp.zeros((8, 128), jnp.int32)
    idv[0, 0:2, 0:8] = ids_in[...]

    greet = [at(dz=1), at(dz=-1), along(1), along(-1)]
    greet += [at(dx=dx, dc=dc) for dx in range(NX) for dc in range(NC) if dx or dc]
    greet += [at(dy=dy, dc=dc) for dy in range(1, NY) for dc in range(NC)]
    barrier = pltpu.get_barrier_semaphore()
    for device in greet:
        pl.semaphore_signal(barrier, inc=1, device_id=device, device_id_type=pl.DeviceIdType.MESH)
    pl.semaphore_wait(barrier, len(greet))

    def z_copy(f, right, k):
        count = BLOCKS if k < 4 else BLOCKS // 2
        shift = 0 if (k < 4 or right) else BLOCKS // 2
        source = (k - 1) if right else (NZ - (k - 1)) % NZ
        target = k if right else NZ - k
        i = (k - 1) if right else 4 + (k - 1)
        return remote(
            pool[f].at[pl.ds(BLOCKS * source + shift, count)],
            pool[f].at[pl.ds(BLOCKS * target + shift, count)],
            z_send.at[f, i], z_recv.at[f, i], at(dz=1 if right else -1),
        )

    def id_copy(dx, dc):
        slot = ((NX - dx) % NX) * 2 + dc
        return remote(idv.at[0], idv.at[slot], id_sem.at[slot], id_sem.at[8 + slot], at(dx=dx, dc=dc))

    def x_first(u, half):
        return remote(
            s1[u].at[half], r1[u].at[half], x_send.at[u, half], x_recv.at[u, half],
            at(dx=2 if u in DIRECT else -1 if half == 0 else 1),
        )

    def x_second(u, right, half):
        i = 2 + 2 * right + half
        return remote(
            s2[u].at[right, half], r2[u].at[right, half], x_send.at[u, i], x_recv.at[u, i],
            at(dx=1 if right else -1),
        )

    def a_ends(u, core, t):
        shared, chunks = UNITS[u]
        where = (
            slice(None), pl.ds(pl.multiple_of(PART * part, PART), PART),
            pl.ds(WIDE * chunks[0], WIDE * len(chunks)),
        )
        if shared:
            return fin[u].at[core, pl.ds(EACH * t, EACH)], nbp.at[where]
        return fin[u].at[core], nbr.at[where]

    def a_copy(u, dy, dc):
        i = dy * 2 + dc
        return remote(*a_ends(u, dc, lax.rem(y + dy, NY)), a_send.at[u, i], a_recv.at[u, i], at(dy=dy, dc=dc))

    def a_local(u):
        return pltpu.make_async_copy(*a_ends(u, 0, y), a_own.at[u])

    def w_place(unit, rel, of=None):
        t = lax.rem(y + rel + NY, NY)
        if unit < 3:
            return wqkv.at[unit, pl.ds(pl.multiple_of(512 * c, 512), 512), pl.ds(pl.multiple_of(256 * t, 256), 256)]
        return wout.at[pl.ds(pl.multiple_of(256 * t + 128 * c, 128), 128)]

    def w_own(unit):
        if unit < 3:
            return enc_qkv.at[unit, pl.ds(pl.multiple_of(512 * c, 512), 512)]
        return enc_out.at[pl.ds(pl.multiple_of(128 * c, 128), 128)]

    def w_first(unit, right):
        i = unit + 4 * right
        return remote(w_own(unit), w_place(unit, 0), w_send.at[i], w_recv.at[i], at(dy=1 if right else -1))

    def w_second(unit):
        right = unit < 2
        return remote(
            w_place(unit, -1 if right else 1), w_place(unit, -1 if right else 1),
            w_send.at[8 + unit], w_recv.at[8 + unit], at(dy=1 if right else -1),
        )

    def w_twin(unit, rel):
        i = unit + 4 * (rel - 1)
        return remote(w_place(unit, rel), w_place(unit, rel), b_send.at[i], b_recv.at[i], at(dc=1))

    def e_slot(m, rel):
        t = lax.rem(y + rel + NY, NY)
        return 3 * t + m + lax.rem(t, 2) * (2 - 2 * m)

    def e_first(m, right):
        i = 2 * m + right
        place = enc.at[e_slot(m, 0)]
        return remote(place, place, e_send.at[i], e_recv.at[i], at(dy=1 if right else -1))

    def e_second(m, right):
        i = 6 + m + (1 if m == 2 and not right else 0)
        rows = pl.ds(0, ROWS) if m < 2 else pl.ds(0 if right else ROWS // 2, ROWS // 2)
        place = enc.at[e_slot(m, -1 if right else 1), rows]
        return remote(place, place, e_send.at[i], e_recv.at[i], at(dy=1 if right else -1))

    def h_query():
        return remote(queries.at[pl.ds(0, M)], halo, h_send.at[0], h_recv.at[0], along(-1))

    def h_back():
        return remote(back_out, back_in, h_send.at[1], h_recv.at[1], along(1))

    def fill_table():
        def step(q, carry):
            for p, j in enumerate(PLACES):
                b = ids_s[q, j % 2, j // 2]
                table[0, q, p] = ((z - (b >> 6) + NZ) & (NZ - 1)) * BLOCKS + (b & (BLOCKS - 1))
                table[1, q, p] = ((b >> 4) - x + NX) & (NX - 1)
            return carry

        lax.fori_loop(0, 8, step, 0)

    def each(u, act):
        shared, chunks = UNITS[u]
        first, count = (0, SHARED // 2) if shared else (SHARED, 2)

        def step(i, carry):
            for core in range(2):
                for n, f in enumerate(chunks):
                    act(f, core, i, (first + i, first + count + i), slice(WIDE * n, WIDE * (n + 1)))
            return carry

        lax.fori_loop(0, count, step, 0, unroll=2)

    def mine(f, requester, core, p):
        return pool[f][table[0, 2 * requester + core, p]]

    def owner(requester, core, p):
        return table[1, 2 * requester + core, p]

    def first_select(u):
        def act(f, core, i, p, cols):
            for half in range(2):
                s1[u][half, core, i, :, cols] = mine(f, 2, core, p[half])

        each(u, act)

    def plain_select(u):
        def act(f, core, i, p, cols):
            s2[u][0, 1, core, i, :, cols] = mine(f, 3, core, p[1])
            s2[u][1, 0, core, i, :, cols] = mine(f, 1, core, p[0])
            if u in DIRECT:
                s2[u][0, 0, core, i, :, cols] = mine(f, 3, core, p[0])
                s2[u][1, 1, core, i, :, cols] = mine(f, 1, core, p[1])

        each(u, act)

    def merge_select(u):
        def act(f, core, i, p, cols):
            s2[u][0, 0, core, i, :, cols] = jnp.where(
                owner(3, core, p[0]) == 0, mine(f, 3, core, p[0]), r1[u][0, core, i, :, cols]
            )
            s2[u][1, 1, core, i, :, cols] = jnp.where(
                owner(1, core, p[1]) == 0, mine(f, 1, core, p[1]), r1[u][1, core, i, :, cols]
            )

        each(u, act)

    def last_select(u):
        count = SHARED // 2 if UNITS[u][0] else 2

        def act(f, core, i, p, cols):
            for half in range(2):
                of = owner(0, core, p[half])
                right, left = r2[u][0, half, core, i, :, cols], r2[u][1, half, core, i, :, cols]
                if u in DIRECT:
                    far = jnp.where(of == 1, right, jnp.where(of == 3, left, r1[u][half, core, i, :, cols]))
                elif half == 0:
                    far = jnp.where(of == 3, left, right)
                else:
                    far = jnp.where(of == 1, right, left)
                fin[u][core, half * count + i, :, cols] = jnp.where(of == 0, mine(f, 0, core, p[half]), far)

        each(u, act)

    def shift_queries():
        top = lax.broadcasted_iota(jnp.int32, (M, D), 0) == 0
        before = jnp.zeros((M, D), F32)
        for g in range(9):
            tile = qraw[pl.ds(M * g, M)] if g < 8 else halo[...]
            turned = pltpu.roll(tile.astype(F32), 1, 0)
            qpad[g] = jnp.where(top, before, turned).astype(BF)
            before = turned

    def gain(ref):
        g = ref[...].astype(F32)
        return jnp.concatenate([g[i : i + 1] for i in range(8)], axis=1)

    def encode_in(blocks, count):
        rows = pl.ds(0, count * ROWS)
        raw = blocks[...].reshape(count * ROWS, D).astype(F32)
        scale = lax.rsqrt(jnp.mean(raw * raw, axis=1, keepdims=True) + EPS)
        normed[rows] = (raw * scale * gain(norm_gain)).astype(BF)

        def project_in(g, carry):
            cols = pl.ds(pl.multiple_of(512 * g, 512), 512)
            for j in range(3):
                qs[j, rows, cols] = jnp.dot(normed[rows], wqkv[j, :, cols], preferred_element_type=F32).astype(BF)
            return carry

        lax.fori_loop(0, 2, project_in, 0)

    def encode_mix(count):
        rows = pl.ds(0, count * ROWS)
        low = lax.broadcasted_iota(jnp.int32, (ROWS, 128), 1) < 64
        zero, one = jnp.zeros((ROWS, 128), BF), jnp.ones((ROWS, 128), BF)
        sums = jnp.concatenate([jnp.where(low, one, zero), jnp.where(low, zero, one)], axis=0)

        def heads(g, carry):
            cols = pl.ds(pl.multiple_of(256 * g, 256), 256)
            q, k, v = qs[0, rows, cols], qs[1, rows, cols], qs[2, rows, cols]
            mixed = []
            for n in range(count):
                pairs = []
                for p in range(2):
                    cut = (slice(ROWS * n, ROWS * (n + 1)), slice(128 * p, 128 * (p + 1)))
                    qp, kp, vp = q[cut], k[cut], v[cut]
                    k2 = jnp.concatenate([jnp.where(low, kp, zero), jnp.where(low, zero, kp)], axis=0)
                    v2 = jnp.concatenate([jnp.where(low, vp, zero), jnp.where(low, zero, vp)], axis=0)
                    s = lax.dot_general(qp, k2, (((1,), (1,)), ((), ())), preferred_element_type=F32)
                    probs = []
                    for h in range(2):
                        sh = s[:, 128 * h : 128 * (h + 1)]
                        top = jnp.max(sh, axis=1, keepdims=True)
                        probs.append(jnp.exp2((sh - top) * (0.125 * LOG2E)).astype(BF))
                    o = jnp.dot(
                        jnp.concatenate(probs, axis=1), jnp.concatenate([v2, sums], axis=1),
                        preferred_element_type=F32,
                    )
                    pairs.append((o[:, :128] / o[:, 128:]).astype(BF))
                mixed.append(jnp.concatenate(pairs, axis=1))
            ctx[rows, cols] = jnp.concatenate(mixed, axis=0)
            return carry

        lax.fori_loop(0, 4, heads, 0, unroll=4)

    def encode_out(blocks, count, places):
        rows = pl.ds(0, count * ROWS)

        def project_out(g, carry):
            cols = pl.ds(pl.multiple_of(512 * g, 512), 512)
            upd[rows, cols] = jnp.dot(ctx[rows], wout[:, cols], preferred_element_type=F32)
            return carry

        lax.fori_loop(0, 2, project_out, 0)
        total = upd[rows] + blocks[...].reshape(count * ROWS, D).astype(F32)
        scale = lax.rsqrt(jnp.mean(total * total, axis=1, keepdims=True) + EPS)
        done = (total * scale * gain(out_gain)).astype(BF)
        for n, place in enumerate(places):
            enc[place] = done[ROWS * n : ROWS * (n + 1)]

    def attend(w):
        rows = enc[pl.ds(2 * w, 2)].reshape(2 * ROWS, D)

        def project(g, carry):
            cols = pl.ds(pl.multiple_of(512 * g, 512), 512)
            for j in range(2):
                kv[j, :, cols] = jnp.dot(rows, wcca[j, :, cols], preferred_element_type=F32).astype(BF)
            return carry

        lax.fori_loop(0, 2, project, 0)
        count = jnp.ones((2 * ROWS, 128), BF)

        def heads(g, carry):
            cols = pl.ds(pl.multiple_of(256 * g, 256), 256)
            q, k, v = qpad[w + 1, :, cols], kv[0, :, cols], kv[1, :, cols]
            mixed = []
            for h in range(2):
                cut = slice(128 * h, 128 * (h + 1))
                s = lax.dot_general(
                    q[:, cut], k[:, cut], (((1,), (1,)), ((), ())), preferred_element_type=F32
                )
                top = jnp.max(s, axis=1, keepdims=True)
                e = jnp.exp2((s - top) * (128.0 ** -0.5 * LOG2E)).astype(BF)
                o = jnp.dot(e, jnp.concatenate([v[:, cut], count], axis=1), preferred_element_type=F32)
                mixed.append((o[:, :128] / o[:, 128:]).astype(BF))
            out[w + 1, :, cols] = jnp.concatenate(mixed, axis=1)
            return carry

        lax.fori_loop(0, 4, heads, 0, unroll=4)

    others = [(dy, dc) for dy in (2, 1, 3, 0) for dc in range(NC) if dy or dc]
    pair, odd = y // 2, lax.rem(y, 2)
    own_base, other_base = 3 * pair, 3 * (1 - pair)

    def z_step(f, k):
        if k == 1:
            own_piece(f).wait()
        else:
            z_copy(f, True, k - 1).wait_recv()
            z_copy(f, False, k - 1).wait_recv()
        go(z_copy(f, True, k))
        go(z_copy(f, False, k))

    def z_done(f):
        z_copy(f, True, 4).wait_recv()
        z_copy(f, False, 4).wait_recv()

    def x_step1(u):
        first_select(u)
        go(x_first(u, 0))
        go(x_first(u, 1))
        plain_select(u)
        go(x_second(u, 0, 1))
        go(x_second(u, 1, 0))
        if u in DIRECT:
            go(x_second(u, 0, 0))
            go(x_second(u, 1, 1))

    def x_step2(u):
        x_first(u, 0).wait_recv()
        x_first(u, 1).wait_recv()
        merge_select(u)
        go(x_second(u, 0, 0))
        go(x_second(u, 1, 1))

    def x_step3(u):
        for right in range(2):
            for half in range(2):
                x_second(u, right, half).wait_recv()
        if u in DIRECT:
            x_first(u, 0).wait_recv()
            x_first(u, 1).wait_recv()
        last_select(u)
        for dy, dc in others:
            go(a_copy(u, dy, dc))
        a_local(u).start()

    def w_start(pos):
        go(w_first(pos, 1))
        go(w_first((pos + 2) % 4, 0))

    def w_forward(pos):
        for right in (1, 0):
            unit = pos if right else (pos + 2) % 4
            w_first(unit, right).wait_recv()
            if pos < 2:
                go(w_second(unit))
            go(w_twin(unit, 3 if right else 1))

    def w_rest(n):
        for unit in (n, n + 2):
            w_second(unit).wait_recv()
            go(w_twin(unit, 2))

    def ids_ready():
        for dx in range(NX):
            for dc in range(NC):
                if dx or dc:
                    id_copy(dx, dc).wait_recv()
        copy = pltpu.make_async_copy(idv, ids_s, id_sem.at[0])
        copy.start()
        copy.wait()
        fill_table()

    def queries_ready():
        local[3].wait()
        h_query().wait_recv()
        shift_queries()

    def blocks_ready(shared):
        for u, unit in enumerate(UNITS):
            if unit[0] == shared:
                for dy, dc in others:
                    a_copy(u, dy, dc).wait_recv()
                a_local(u).wait()

    def e_send_both(m):
        go(e_first(m, 1))
        go(e_first(m, 0))

    def encode_own(stage):
        if stage == 0:
            blocks_ready(1)
            for rel in range(1, 4):
                for unit in range(4):
                    w_twin(unit, rel).wait_recv()
            for i in range(3):
                local[i].wait()
            first = nbp.at[pl.ds(0, 1)]
            encode_in(first, 1)
            encode_mix(1)
            encode_out(first, 1, [e_slot(0, 0)])
            e_send_both(0)
        rest = nbp.at[pl.ds(1, 2)]
        if stage == 1:
            encode_in(rest, 2)
        elif stage == 2:
            encode_mix(2)
        elif stage == 3:
            encode_out(rest, 2, [e_slot(1, 0), e_slot(2, 0)])
            e_send_both(1)
            e_send_both(2)

    def encode_common(i, stage):
        blocks = nbr.at[pl.ds(2 * i, 2)]
        if stage == 0:
            if i == 0:
                blocks_ready(0)
            encode_in(blocks, 2)
        elif stage == 1:
            encode_mix(2)
        else:
            encode_out(blocks, 2, [SHARED + 2 * i, SHARED + 2 * i + 1])

    def e_forward(m):
        if m != 1:
            e_first(m, 1).wait_recv()
            go(e_second(m, True))
        if m != 0:
            e_first(m, 0).wait_recv()
            go(e_second(m, False))

    def e_near():
        e_first(0, 0).wait_recv()
        e_first(1, 1).wait_recv()

    def attend_step(n):
        if n == 4:
            e_second(0, True).wait_recv()
            e_second(1, False).wait_recv()
        if n == 5:
            e_second(2, True).wait_recv()
            e_second(2, False).wait_recv()
        attend((
            own_base + 2 * odd, own_base + 2 * (1 - odd), other_base + 2 * (1 - odd), own_base + 1,
            other_base + 2 * odd, other_base + 1, 6, 7,
        )[n])

    def give_back():
        back_out[...] = out[8]
        go(h_back())

    steps = dict(
        z=z_step, zd=z_done, x1=x_step1, x2=x_step2, x3=x_step3, w0=w_start, wf=w_forward, wr=w_rest, q=queries_ready,
        ids=ids_ready, en=encode_own, er=encode_common, ef=e_forward, ar=e_near, at=attend_step, hb=give_back,
    )
    for dx in range(NX):
        for dc in range(NC):
            if dx or dc:
                go(id_copy(dx, dc))
    go(h_query())
    for name, *which in ORDER:
        steps[name](*which)
    h_back().wait_recv()
    out[0] = back_in[...]
    for copy in started:
        copy.wait_send()


def fused(ids, queries, database, norm_gain, enc_qkv, enc_out, out_gain, cca_kv):
    dma = pltpu.SemaphoreType.DMA
    NU = len(UNITS)
    def per_unit(*lead):
        return [
            pltpu.VMEM(lead + (SHARED // 2 if shared else 2, PART, WIDE * len(chunks)), BF)
            for shared, chunks in UNITS
        ]

    scratch = [pltpu.VMEM((NZ * BLOCKS, PART, WIDE), BF) for _ in range(NF)]
    scratch += per_unit(2, 2) + per_unit(2, 2) + per_unit(2, 2, 2) + per_unit(2, 2, 2)
    scratch += [
        pltpu.VMEM((2, SHARED if shared else 4, PART, WIDE * len(chunks)), BF) for shared, chunks in UNITS
    ]
    scratch += [
        pltpu.VMEM((8, 8, 128), jnp.int32),
        pltpu.SMEM((8, 8, 128), jnp.int32),
        pltpu.SMEM((2, 8, 16), jnp.int32),
        pltpu.VMEM((EACH, ROWS, D), BF),
        pltpu.VMEM((4, ROWS, D), BF),
        pltpu.VMEM((3, D, D), BF),
        pltpu.VMEM((D, D), BF),
        pltpu.VMEM((2, D, D), BF),
        pltpu.VMEM((SLOTS, ROWS, D), BF),
        pltpu.VMEM((8 * M, D), BF),
        pltpu.VMEM((M, D), BF),
        pltpu.VMEM((9, M, D), BF),
        pltpu.VMEM((M, D), BF),
        pltpu.VMEM((M, D), BF),
        pltpu.VMEM((2 * ROWS, D), BF),
        pltpu.VMEM((2 * ROWS, D), BF),
        pltpu.VMEM((2 * ROWS, D), F32),
        pltpu.VMEM((3, 2 * ROWS, D), BF),
        pltpu.VMEM((2, 2 * ROWS, D), BF),
        dma((16,)), dma((NF + 4,)), dma((NF, 8)), dma((NF, 8)), dma((NU, 6)), dma((NU, 6)),
        dma((NU, 8)), dma((NU, 8)), dma((NU,)),
        dma((12,)), dma((12,)), dma((12,)), dma((12,)), dma((10,)), dma((10,)), dma((2,)), dma((2,)),
    ]
    vmem = pl.BlockSpec(memory_space=pltpu.VMEM)
    hbm = pl.BlockSpec(memory_space=pl.ANY)
    return pl.pallas_call(
        body,
        out_shape=jax.ShapeDtypeStruct((9, M, D), BF),
        in_specs=[vmem, hbm, hbm, vmem, hbm, hbm, vmem, hbm],
        out_specs=vmem,
        scratch_shapes=scratch,
        compiler_params=pltpu.CompilerParams(
            collective_id=0, has_side_effects=True, vmem_limit_bytes=56 * 2**20
        ),
        cost_estimate=pl.CostEstimate(flops=14 * 10**9, bytes_accessed=12 * 2**20, transcendentals=4 * 10**6),
    )(ids, queries, database, norm_gain, enc_qkv, enc_out, out_gain, cca_kv)


def per_device(queries, database, nbr_ids, norm_gain, enc_qkv, enc_out, out_gain, cca_kv):
    groups = fused(
        nbr_ids.T, queries, database, norm_gain.reshape(8, 128), enc_qkv, enc_out, out_gain.reshape(8, 128), cca_kv
    )
    tokens = queries.shape[0]
    attended = groups.reshape(9 * M, D)[1 : tokens + 1]
    unserved = (lax.axis_index("seq") == 0) & (lax.broadcasted_iota(jnp.int32, (tokens, 1), 0) < M - 1)
    return jnp.where(unserved, jnp.zeros((), BF), attended)


def solution(mesh):
    placed = (
        P(("dp", "seq"), "tensor"),
        P("seq", None, None),
        P(("dp", "seq"), None),
        P(),
        P(None, None, "tensor"),
        P("tensor", None),
        P(),
        P(None, None, "tensor"),
    )
    return jax.shard_map(
        per_device,
        mesh=mesh,
        in_specs=placed,
        out_specs=P(("dp", "seq"), "tensor"),
        check_vma=False,
    )
```

time: 149 us -> 115 us (0.77)
  Pallas kernels: 142 us -> 113 us
  local copies, waits for them, and re-layouts: 3.89 us -> 0 us
    pallas_call x1, Pallas kernels: 142 us -> 113 us  [fused(): pl.pallas_call(body, out_shape=jax.ShapeDtypeStruct((9, M, D), BF), in_sp...]
    reshape x2 -> x0, local copies, waits for them, and re-layouts: 2.55 us -> none  [the longest x1 1.27 us: per_device(): norm_gain.reshape(1, D)]
where the time goes in v2:
time: 115 us
  Pallas kernels  113 us (98%)
  other arithmetic  2.52 us (2%)
    pallas_call x1, Pallas kernels, fused(): pl.pallas_call(body, out_shape=jax.ShapeDtypeStruct((9, M, D), BF), in_sp...  113 us
    select_n x1, other arithmetic, per_device(): return jnp.where(unserved, jnp.zeros((), BF), attended)  2.52 us

profile of v2, /device:TPU:1, one launch (start us, length us, event | category | flops | bytes accessed | tf_op | source)
XLA Modules:
  0.0 115.2 jit_solution(590802321592916459)
XLA Ops:
  0.0 112.7 %shard_map.82 = bf16[9,64,1024]{2,1,0:T(8,128)(2,1)} custom-call(s32[2,8]{1,0:T(2,128)} %bitcast.7, bf16[512,1024]{1,0:T(8,128)(2,1)} %queries.1, bf16[16,128,1024]{2,1,0:T(8,128)(2,1)} %database.1, bf16[8,128]{1,0:T(8,128)(2,1)} %bitcast.5, bf16[3,1024,256]{2,1,0:T(8,128)(2,1)} %enc_qkv.1, bf16[256,1024]{1,0:T(8,128)(2,1)} %enc_out.1, ...), custom_call_target="tpu_custom_call" | custom-call | flops 14000000000 | bytes 12582912 | tf_op jit(solution)/shard_map/pallas_call | solution.py:607
  112.7 2.5 %slice_select_fusion = bf16[512,1024]{1,0:T(8,128)(2,1)} fusion(bf16[576,1024]{1,0:T(8,128)(2,1)} %bitcast.4, pred[512]{0:T(512)(128)(4,1)S(1)} %fusion), kind=kLoop, calls=%fused_computation | loop fusion | flops 524288 | bytes 2097664 | tf_op jit(solution)/shard_map/jit(_where)/select_n | solution.py:627
  (1 shorter events, 0.0 us)

commit v3 on v2

--- a/solution.py
+++ b/solution.py
@@ -17,28 +17,29 @@
 EPS = 1e-6
 NF = 8
 WIDE = D // NF
-UNITS = ((1, (0, 1)), (1, (2, 3)), (1, (4, 5)), (1, (6,)), (1, (7,)), (0, (0, 1, 2, 3)), (0, (4, 5, 6, 7)))
-DIRECT = ()
-SHARED = 12
+UNITS = ((1, (0, 1)), (1, (2, 3)), (1, (4, 5)), (1, (6, 7)), (0, (0, 1)), (0, (2, 3)), (0, (4, 5)), (0, (6, 7)))
+SHARED = 8
 EACH = SHARED // NY
-PLACES = tuple(3 * t + (m if t % 2 == 0 else 2 - m) for t in range(NY) for m in range(EACH)) + (12, 13, 14, 15)
+HALF = 4
 ORDER = (
-    ('z', 2, 1), ('z', 0, 1), ('z', 1, 1), ('z', 3, 1), ('z', 0, 2), ('w0', 0),
-    ('z', 1, 2), ('z', 2, 2), ('z', 3, 2), ('w0', 1), ('z', 0, 3), ('z', 1, 3),
-    ('w0', 2), ('z', 3, 3), ('ids',), ('z', 0, 4), ('z', 2, 3), ('z', 1, 4),
-    ('z', 4, 1), ('zd', 0), ('z', 7, 1), ('z', 2, 4), ('z', 3, 4), ('z', 5, 1),
-    ('zd', 1), ('x1', 0), ('z', 4, 2), ('wf', 0), ('z', 7, 2), ('zd', 2),
-    ('zd', 3), ('x1', 1), ('z', 6, 1), ('x2', 0), ('z', 5, 2), ('wf', 1),
-    ('z', 7, 3), ('x1', 5), ('z', 4, 3), ('z', 5, 3), ('x2', 1), ('z', 7, 4),
-    ('w0', 3), ('z', 6, 2), ('x3', 0), ('z', 4, 4), ('x2', 5), ('z', 5, 4),
-    ('wr', 0), ('zd', 7), ('x1', 4), ('z', 6, 3), ('zd', 4), ('zd', 5),
-    ('x1', 2), ('wr', 1), ('z', 6, 4), ('x3', 1), ('x2', 4), ('x2', 2),
-    ('zd', 6), ('x1', 3), ('wf', 2), ('x3', 5), ('x1', 6), ('q',),
-    ('x2', 3), ('x3', 2), ('x2', 6), ('x3', 4), ('wf', 3), ('x3', 3),
-    ('x3', 6), ('en', 0), ('en', 1), ('en', 2), ('en', 3), ('er', 0, 0),
-    ('er', 0, 1), ('er', 0, 2), ('ef', 0), ('er', 1, 0), ('er', 1, 1), ('er', 1, 2),
-    ('at', 6), ('ef', 1), ('at', 7), ('hb',), ('at', 0), ('ar',),
-    ('at', 1), ('ef', 2), ('at', 2), ('at', 3), ('at', 4), ('at', 5),
+    ('z', 5, 1), ('w0', 0), ('z', 2, 1), ('z', 3, 1), ('w0', 2), ('ids',),
+    ('q',), ('z', 1, 1), ('w0', 1), ('z', 2, 2), ('z', 3, 2), ('z', 0, 1),
+    ('z', 2, 3), ('wf', 0), ('z', 3, 3), ('z', 0, 2), ('z', 1, 2), ('z', 3, 4),
+    ('z', 2, 4), ('z', 0, 3), ('z', 1, 3), ('qw', 3), ('z', 4, 1), ('w0', 3),
+    ('zd', 3), ('zd', 2), ('z', 5, 2), ('x1', 1), ('x1', 5), ('wf', 1),
+    ('z', 1, 4), ('z', 0, 4), ('z', 4, 2), ('z', 7, 1), ('qw', 0), ('x2', 1),
+    ('zd', 1), ('wf', 2), ('z', 5, 3), ('x2', 5), ('zd', 0), ('z', 4, 3),
+    ('x1', 4), ('z', 6, 1), ('z', 7, 2), ('x1', 0), ('z', 5, 4), ('x3', 5),
+    ('x2', 4), ('z', 4, 4), ('z', 6, 2), ('x3', 1), ('x2', 0), ('z', 7, 3),
+    ('zd', 5), ('wf', 3), ('zd', 4), ('x1', 6), ('z', 6, 3), ('x1', 2),
+    ('x3', 4), ('wr', 1), ('z', 7, 4), ('x2', 6), ('z', 6, 4), ('x3', 0),
+    ('x2', 2), ('zd', 6), ('zd', 7), ('x1', 3), ('x3', 6), ('x1', 7),
+    ('x2', 3), ('x3', 2), ('qw', 1), ('x2', 7), ('qw', 2), ('wr', 0),
+    ('x3', 3), ('x3', 7), ('en', 0), ('en', 1), ('en', 2), ('at', 0),
+    ('er', 0, 0), ('er', 0, 1), ('er', 0, 2), ('er', 1, 0), ('er', 1, 1), ('er', 1, 2),
+    ('ef', 0), ('ef', 1), ('er', 2, 0), ('er', 2, 1), ('er', 2, 2), ('at', 5),
+    ('er', 3, 0), ('er', 3, 1), ('er', 3, 2), ('at', 7), ('hb',), ('at', 2),
+    ('at', 3), ('at', 1), ('at', 4), ('at', 6),
 )
 LOG2E = 1.4426950408889634
 BF = jnp.bfloat16
@@ -61,7 +62,7 @@
     s1, r1, s2, r2, fin = (take(len(UNITS)) for _ in range(5))
     (
         idv, ids_s, table, nbp, nbr, wqkv, wout, wcca, enc, qraw, halo, qpad, back_out, back_in,
-        normed, ctx, upd, qs, kv,
+        normed, ctx, upd, qs, values, qw,
         id_sem, load_sem, z_send, z_recv, x_send, x_recv, a_send, a_recv, a_own,
         w_send, w_recv, b_send, b_recv, e_send, e_recv, h_send, h_recv,
     ) = scratch
@@ -142,7 +143,7 @@
     def x_first(u, half):
         return remote(
             s1[u].at[half], r1[u].at[half], x_send.at[u, half], x_recv.at[u, half],
-            at(dx=2 if u in DIRECT else -1 if half == 0 else 1),
+            at(dx=-1 if half == 0 else 1),
         )
 
     def x_second(u, right, half):
@@ -195,20 +196,16 @@
         i = unit + 4 * (rel - 1)
         return remote(w_place(unit, rel), w_place(unit, rel), b_send.at[i], b_recv.at[i], at(dc=1))
 
-    def e_slot(m, rel):
-        t = lax.rem(y + rel + NY, NY)
-        return 3 * t + m + lax.rem(t, 2) * (2 - 2 * m)
+    def e_place(m, rel):
+        return enc.at[2 * lax.rem(y + rel + NY, NY) + m]
 
     def e_first(m, right):
         i = 2 * m + right
-        place = enc.at[e_slot(m, 0)]
-        return remote(place, place, e_send.at[i], e_recv.at[i], at(dy=1 if right else -1))
-
-    def e_second(m, right):
-        i = 6 + m + (1 if m == 2 and not right else 0)
-        rows = pl.ds(0, ROWS) if m < 2 else pl.ds(0 if right else ROWS // 2, ROWS // 2)
-        place = enc.at[e_slot(m, -1 if right else 1), rows]
-        return remote(place, place, e_send.at[i], e_recv.at[i], at(dy=1 if right else -1))
+        return remote(e_place(m, 0), e_place(m, 0), e_send.at[i], e_recv.at[i], at(dy=1 if right else -1))
+
+    def e_second(m):
+        rel = -1 if m == 0 else 1
+        return remote(e_place(m, rel), e_place(m, rel), e_send.at[4 + m], e_recv.at[4 + m], at(dy=-rel))
 
     def h_query():
         return remote(queries.at[pl.ds(0, M)], halo, h_send.at[0], h_recv.at[0], along(-1))
@@ -218,8 +215,8 @@
 
     def fill_table():
         def step(q, carry):
-            for p, j in enumerate(PLACES):
-                b = ids_s[q, j % 2, j // 2]
+            for p in range(SLOTS):
+                b = ids_s[q, p % 2, p // 2]
                 table[0, q, p] = ((z - (b >> 6) + NZ) & (NZ - 1)) * BLOCKS + (b & (BLOCKS - 1))
                 table[1, q, p] = ((b >> 4) - x + NX) & (NX - 1)
             return carry
@@ -228,15 +225,15 @@
 
     def each(u, act):
         shared, chunks = UNITS[u]
-        first, count = (0, SHARED // 2) if shared else (SHARED, 2)
+        first = 0 if shared else SHARED
 
         def step(i, carry):
             for core in range(2):
                 for n, f in enumerate(chunks):
-                    act(f, core, i, (first + i, first + count + i), slice(WIDE * n, WIDE * (n + 1)))
+                    act(f, core, i, (first + i, first + HALF + i), slice(WIDE * n, WIDE * (n + 1)))
             return carry
 
-        lax.fori_loop(0, count, step, 0, unroll=2)
+        lax.fori_loop(0, HALF, step, 0, unroll=2)
 
     def mine(f, requester, core, p):
         return pool[f][table[0, 2 * requester + core, p]]
@@ -255,9 +252,6 @@
         def act(f, core, i, p, cols):
             s2[u][0, 1, core, i, :, cols] = mine(f, 3, core, p[1])
             s2[u][1, 0, core, i, :, cols] = mine(f, 1, core, p[0])
-            if u in DIRECT:
-                s2[u][0, 0, core, i, :, cols] = mine(f, 3, core, p[0])
-                s2[u][1, 1, core, i, :, cols] = mine(f, 1, core, p[1])
 
         each(u, act)
 
@@ -273,19 +267,15 @@
         each(u, act)
 
     def last_select(u):
-        count = SHARED // 2 if UNITS[u][0] else 2
-
         def act(f, core, i, p, cols):
             for half in range(2):
                 of = owner(0, core, p[half])
                 right, left = r2[u][0, half, core, i, :, cols], r2[u][1, half, core, i, :, cols]
-                if u in DIRECT:
-                    far = jnp.where(of == 1, right, jnp.where(of == 3, left, r1[u][half, core, i, :, cols]))
-                elif half == 0:
+                if half == 0:
                     far = jnp.where(of == 3, left, right)
                 else:
                     far = jnp.where(of == 1, right, left)
-                fin[u][core, half * count + i, :, cols] = jnp.where(of == 0, mine(f, 0, core, p[half]), far)
+                fin[u][core, half * HALF + i, :, cols] = jnp.where(of == 0, mine(f, 0, core, p[half]), far)
 
         each(u, act)
 
@@ -308,13 +298,8 @@
         scale = lax.rsqrt(jnp.mean(raw * raw, axis=1, keepdims=True) + EPS)
         normed[rows] = (raw * scale * gain(norm_gain)).astype(BF)
 
-        def project_in(g, carry):
-            cols = pl.ds(pl.multiple_of(512 * g, 512), 512)
-            for j in range(3):
-                qs[j, rows, cols] = jnp.dot(normed[rows], wqkv[j, :, cols], preferred_element_type=F32).astype(BF)
-            return carry
-
-        lax.fori_loop(0, 2, project_in, 0)
+        for j in range(3):
+            qs[j, rows] = jnp.dot(normed[rows], wqkv[j], preferred_element_type=F32).astype(BF)
 
     def encode_mix(count):
         rows = pl.ds(0, count * ROWS)
@@ -353,51 +338,39 @@
     def encode_out(blocks, count, places):
         rows = pl.ds(0, count * ROWS)
 
-        def project_out(g, carry):
-            cols = pl.ds(pl.multiple_of(512 * g, 512), 512)
-            upd[rows, cols] = jnp.dot(ctx[rows], wout[:, cols], preferred_element_type=F32)
-            return carry
-
-        lax.fori_loop(0, 2, project_out, 0)
+        upd[rows] = jnp.dot(ctx[rows], wout[...], preferred_element_type=F32)
         total = upd[rows] + blocks[...].reshape(count * ROWS, D).astype(F32)
         scale = lax.rsqrt(jnp.mean(total * total, axis=1, keepdims=True) + EPS)
         done = (total * scale * gain(out_gain)).astype(BF)
         for n, place in enumerate(places):
             enc[place] = done[ROWS * n : ROWS * (n + 1)]
 
+    def fold_keys(i):
+        rows = qpad[pl.ds(2 * i + 1, 2)].reshape(2 * M, D)
+        for h in range(8):
+            cut = slice(128 * h, 128 * (h + 1))
+            folded = lax.dot_general(
+                rows[:, cut], wcca[0, :, cut], (((1,), (1,)), ((), ())), preferred_element_type=F32
+            ).astype(BF)
+            qw[2 * i, M * h : M * (h + 1)] = folded[:M]
+            qw[2 * i + 1, M * h : M * (h + 1)] = folded[M:]
+
     def attend(w):
         rows = enc[pl.ds(2 * w, 2)].reshape(2 * ROWS, D)
-
-        def project(g, carry):
-            cols = pl.ds(pl.multiple_of(512 * g, 512), 512)
-            for j in range(2):
-                kv[j, :, cols] = jnp.dot(rows, wcca[j, :, cols], preferred_element_type=F32).astype(BF)
-            return carry
-
-        lax.fori_loop(0, 2, project, 0)
-        count = jnp.ones((2 * ROWS, 128), BF)
-
-        def heads(g, carry):
-            cols = pl.ds(pl.multiple_of(256 * g, 256), 256)
-            q, k, v = qpad[w + 1, :, cols], kv[0, :, cols], kv[1, :, cols]
-            mixed = []
-            for h in range(2):
-                cut = slice(128 * h, 128 * (h + 1))
-                s = lax.dot_general(
-                    q[:, cut], k[:, cut], (((1,), (1,)), ((), ())), preferred_element_type=F32
-                )
-                top = jnp.max(s, axis=1, keepdims=True)
-                e = jnp.exp2((s - top) * (128.0 ** -0.5 * LOG2E)).astype(BF)
-                o = jnp.dot(e, jnp.concatenate([v[:, cut], count], axis=1), preferred_element_type=F32)
-                mixed.append((o[:, :128] / o[:, 128:]).astype(BF))
-            out[w + 1, :, cols] = jnp.concatenate(mixed, axis=1)
-            return carry
-
-        lax.fori_loop(0, 4, heads, 0, unroll=4)
+        s = lax.dot_general(qw[w], rows, (((1,), (1,)), ((), ())), preferred_element_type=F32)
+        values[...] = jnp.dot(rows, wcca[1], preferred_element_type=F32).astype(BF)
+        top = jnp.max(s, axis=1, keepdims=True)
+        e = jnp.exp2((s - top) * (128.0 ** -0.5 * LOG2E)).astype(BF)
+        sums = jnp.ones((2 * ROWS, 128), BF)
+        for h in range(8):
+            cut = slice(128 * h, 128 * (h + 1))
+            o = jnp.dot(
+                e[M * h : M * (h + 1)], jnp.concatenate([values[:, cut], sums], axis=1),
+                preferred_element_type=F32,
+            )
+            out[w + 1, :, cut] = (o[:, :128] / o[:, 128:]).astype(BF)
 
     others = [(dy, dc) for dy in (2, 1, 3, 0) for dc in range(NC) if dy or dc]
-    pair, odd = y // 2, lax.rem(y, 2)
-    own_base, other_base = 3 * pair, 3 * (1 - pair)
 
     def z_step(f, k):
         if k == 1:
@@ -419,9 +392,6 @@
         plain_select(u)
         go(x_second(u, 0, 1))
         go(x_second(u, 1, 0))
-        if u in DIRECT:
-            go(x_second(u, 0, 0))
-            go(x_second(u, 1, 1))
 
     def x_step2(u):
         x_first(u, 0).wait_recv()
@@ -434,9 +404,6 @@
         for right in range(2):
             for half in range(2):
                 x_second(u, right, half).wait_recv()
-        if u in DIRECT:
-            x_first(u, 0).wait_recv()
-            x_first(u, 1).wait_recv()
         last_select(u)
         for dy, dc in others:
             go(a_copy(u, dy, dc))
@@ -470,6 +437,7 @@
         fill_table()
 
     def queries_ready():
+        local[2].wait()
         local[3].wait()
         h_query().wait_recv()
         shift_queries()
@@ -481,32 +449,21 @@
                     a_copy(u, dy, dc).wait_recv()
                 a_local(u).wait()
 
-    def e_send_both(m):
-        go(e_first(m, 1))
-        go(e_first(m, 0))
-
     def encode_own(stage):
         if stage == 0:
             blocks_ready(1)
             for rel in range(1, 4):
                 for unit in range(4):
                     w_twin(unit, rel).wait_recv()
-            for i in range(3):
+            for i in range(2):
                 local[i].wait()
-            first = nbp.at[pl.ds(0, 1)]
-            encode_in(first, 1)
-            encode_mix(1)
-            encode_out(first, 1, [e_slot(0, 0)])
-            e_send_both(0)
-        rest = nbp.at[pl.ds(1, 2)]
-        if stage == 1:
-            encode_in(rest, 2)
-        elif stage == 2:
+            encode_in(nbp, 2)
+        elif stage == 1:
             encode_mix(2)
-        elif stage == 3:
-            encode_out(rest, 2, [e_slot(1, 0), e_slot(2, 0)])
-            e_send_both(1)
-            e_send_both(2)
+        else:
+            encode_out(nbp, 2, [2 * y, 2 * y + 1])
+            for m, right in ((0, 1), (1, 0), (1, 1), (0, 0)):
+                go(e_first(m, right))
 
     def encode_common(i, stage):
         blocks = nbr.at[pl.ds(2 * i, 2)]
@@ -520,28 +477,18 @@
             encode_out(blocks, 2, [SHARED + 2 * i, SHARED + 2 * i + 1])
 
     def e_forward(m):
-        if m != 1:
-            e_first(m, 1).wait_recv()
-            go(e_second(m, True))
-        if m != 0:
-            e_first(m, 0).wait_recv()
-            go(e_second(m, False))
-
-    def e_near():
-        e_first(0, 0).wait_recv()
-        e_first(1, 1).wait_recv()
+        e_first(m, 1 - m).wait_recv()
+        go(e_second(m))
 
     def attend_step(n):
-        if n == 4:
-            e_second(0, True).wait_recv()
-            e_second(1, False).wait_recv()
-        if n == 5:
-            e_second(2, True).wait_recv()
-            e_second(2, False).wait_recv()
-        attend((
-            own_base + 2 * odd, own_base + 2 * (1 - odd), other_base + 2 * (1 - odd), own_base + 1,
-            other_base + 2 * odd, other_base + 1, 6, 7,
-        )[n])
+        if n == 1:
+            e_first(1, 1).wait_recv()
+        elif n == 2:
+            e_first(0, 0).wait_recv()
+        elif n == 3:
+            e_second(0).wait_recv()
+            e_second(1).wait_recv()
+        attend((y, lax.rem(y + 3, NY), lax.rem(y + 1, NY), lax.rem(y + 2, NY), 4, 5, 6, 7)[n])
 
     def give_back():
         back_out[...] = out[8]
@@ -549,7 +496,7 @@
 
     steps = dict(
         z=z_step, zd=z_done, x1=x_step1, x2=x_step2, x3=x_step3, w0=w_start, wf=w_forward, wr=w_rest, q=queries_ready,
-        ids=ids_ready, en=encode_own, er=encode_common, ef=e_forward, ar=e_near, at=attend_step, hb=give_back,
+        qw=fold_keys, ids=ids_ready, en=encode_own, er=encode_common, ef=e_forward, at=attend_step, hb=give_back,
     )
     for dx in range(NX):
         for dc in range(NC):
@@ -569,21 +516,20 @@
     NU = len(UNITS)
     def per_unit(*lead):
         return [
-            pltpu.VMEM(lead + (SHARED // 2 if shared else 2, PART, WIDE * len(chunks)), BF)
-            for shared, chunks in UNITS
+            pltpu.VMEM(lead + (HALF, PART, WIDE * len(chunks)), BF) for _, chunks in UNITS
         ]
 
     scratch = [pltpu.VMEM((NZ * BLOCKS, PART, WIDE), BF) for _ in range(NF)]
     scratch += per_unit(2, 2) + per_unit(2, 2) + per_unit(2, 2, 2) + per_unit(2, 2, 2)
     scratch += [
-        pltpu.VMEM((2, SHARED if shared else 4, PART, WIDE * len(chunks)), BF) for shared, chunks in UNITS
+        pltpu.VMEM((2, 2 * HALF, PART, WIDE * len(chunks)), BF) for _, chunks in UNITS
     ]
     scratch += [
         pltpu.VMEM((8, 8, 128), jnp.int32),
         pltpu.SMEM((8, 8, 128), jnp.int32),
         pltpu.SMEM((2, 8, 16), jnp.int32),
         pltpu.VMEM((EACH, ROWS, D), BF),
-        pltpu.VMEM((4, ROWS, D), BF),
+        pltpu.VMEM((SLOTS - SHARED, ROWS, D), BF),
         pltpu.VMEM((3, D, D), BF),
         pltpu.VMEM((D, D), BF),
         pltpu.VMEM((2, D, D), BF),
@@ -597,10 +543,11 @@
         pltpu.VMEM((2 * ROWS, D), BF),
         pltpu.VMEM((2 * ROWS, D), F32),
         pltpu.VMEM((3, 2 * ROWS, D), BF),
-        pltpu.VMEM((2, 2 * ROWS, D), BF),
+        pltpu.VMEM((2 * ROWS, D), BF),
+        pltpu.VMEM((8, 8 * M, D), BF),
         dma((16,)), dma((NF + 4,)), dma((NF, 8)), dma((NF, 8)), dma((NU, 6)), dma((NU, 6)),
         dma((NU, 8)), dma((NU, 8)), dma((NU,)),
-        dma((12,)), dma((12,)), dma((12,)), dma((12,)), dma((10,)), dma((10,)), dma((2,)), dma((2,)),
+        dma((12,)), dma((12,)), dma((12,)), dma((12,)), dma((6,)), dma((6,)), dma((2,)), dma((2,)),
     ]
     vmem = pl.BlockSpec(memory_space=pltpu.VMEM)
     hbm = pl.BlockSpec(memory_space=pl.ANY)
@@ -611,7 +558,7 @@
         out_specs=vmem,
         scratch_shapes=scratch,
         compiler_params=pltpu.CompilerParams(
-            collective_id=0, has_side_effects=True, vmem_limit_bytes=56 * 2**20
+            collective_id=0, has_side_effects=True, vmem_limit_bytes=60 * 2**20
         ),
         cost_estimate=pl.CostEstimate(flops=14 * 10**9, bytes_accessed=12 * 2**20, transcendentals=4 * 10**6),
     )(ids, queries, database, norm_gain, enc_qkv, enc_out, out_gain, cca_kv)

time: 115 us -> 108 us (0.939)
  Pallas kernels: 113 us -> 105 us
    pallas_call x1, Pallas kernels: 113 us -> 105 us  [fused(): pl.pallas_call(body, out_shape=jax.ShapeDtypeStruct((9, M, D), BF), in_sp...]
where the time goes in v3:
time: 108 us
  Pallas kernels  105 us (97%)
  other arithmetic  2.52 us (2%)
    pallas_call x1, Pallas kernels, fused(): pl.pallas_call(body, out_shape=jax.ShapeDtypeStruct((9, M, D), BF), in_sp...  105 us
    select_n x1, other arithmetic, per_device(): return jnp.where(unserved, jnp.zeros((), BF), attended)  2.52 us

profile of v3, /device:TPU:1, one launch (start us, length us, event | category | flops | bytes accessed | tf_op | source)
XLA Modules:
  0.0 107.7 jit_solution(11856529877269154796)
XLA Ops:
  0.0 105.2 %shard_map.82 = bf16[9,64,1024]{2,1,0:T(8,128)(2,1)} custom-call(s32[2,8]{1,0:T(2,128)} %bitcast.7, bf16[512,1024]{1,0:T(8,128)(2,1)} %queries.1, bf16[16,128,1024]{2,1,0:T(8,128)(2,1)} %database.1, bf16[8,128]{1,0:T(8,128)(2,1)} %bitcast.5, bf16[3,1024,256]{2,1,0:T(8,128)(2,1)} %enc_qkv.1, bf16[256,1024]{1,0:T(8,128)(2,1)} %enc_out.1, ...), custom_call_target="tpu_custom_call" | custom-call | flops 14000000000 | bytes 12582912 | tf_op jit(solution)/shard_map/pallas_call | solution.py:554
  105.2 2.5 %slice_select_fusion = bf16[512,1024]{1,0:T(8,128)(2,1)} fusion(bf16[576,1024]{1,0:T(8,128)(2,1)} %bitcast.4, pred[512]{0:T(512)(128)(4,1)S(1)} %fusion), kind=kLoop, calls=%fused_computation | loop fusion | flops 524288 | bytes 2097664 | tf_op jit(solution)/shard_map/jit(_where)/select_n | solution.py:574
  (1 shorter events, 0.0 us)

commit v4 on v3

--- a/solution.py
+++ b/solution.py
@@ -22,24 +22,25 @@
 EACH = SHARED // NY
 HALF = 4
 ORDER = (
-    ('z', 5, 1), ('w0', 0), ('z', 2, 1), ('z', 3, 1), ('w0', 2), ('ids',),
-    ('q',), ('z', 1, 1), ('w0', 1), ('z', 2, 2), ('z', 3, 2), ('z', 0, 1),
-    ('z', 2, 3), ('wf', 0), ('z', 3, 3), ('z', 0, 2), ('z', 1, 2), ('z', 3, 4),
-    ('z', 2, 4), ('z', 0, 3), ('z', 1, 3), ('qw', 3), ('z', 4, 1), ('w0', 3),
-    ('zd', 3), ('zd', 2), ('z', 5, 2), ('x1', 1), ('x1', 5), ('wf', 1),
-    ('z', 1, 4), ('z', 0, 4), ('z', 4, 2), ('z', 7, 1), ('qw', 0), ('x2', 1),
-    ('zd', 1), ('wf', 2), ('z', 5, 3), ('x2', 5), ('zd', 0), ('z', 4, 3),
-    ('x1', 4), ('z', 6, 1), ('z', 7, 2), ('x1', 0), ('z', 5, 4), ('x3', 5),
-    ('x2', 4), ('z', 4, 4), ('z', 6, 2), ('x3', 1), ('x2', 0), ('z', 7, 3),
-    ('zd', 5), ('wf', 3), ('zd', 4), ('x1', 6), ('z', 6, 3), ('x1', 2),
-    ('x3', 4), ('wr', 1), ('z', 7, 4), ('x2', 6), ('z', 6, 4), ('x3', 0),
-    ('x2', 2), ('zd', 6), ('zd', 7), ('x1', 3), ('x3', 6), ('x1', 7),
-    ('x2', 3), ('x3', 2), ('qw', 1), ('x2', 7), ('qw', 2), ('wr', 0),
-    ('x3', 3), ('x3', 7), ('en', 0), ('en', 1), ('en', 2), ('at', 0),
-    ('er', 0, 0), ('er', 0, 1), ('er', 0, 2), ('er', 1, 0), ('er', 1, 1), ('er', 1, 2),
-    ('ef', 0), ('ef', 1), ('er', 2, 0), ('er', 2, 1), ('er', 2, 2), ('at', 5),
-    ('er', 3, 0), ('er', 3, 1), ('er', 3, 2), ('at', 7), ('hb',), ('at', 2),
-    ('at', 3), ('at', 1), ('at', 4), ('at', 6),
+    ('z', 5, 1), ('w0', 0), ('z', 2, 1), ('g', 0), ('z', 3, 1), ('w0', 2),
+    ('z', 1, 1), ('w0', 1), ('z', 2, 2), ('g', 1), ('z', 3, 2), ('z', 0, 1),
+    ('g', 2), ('z', 2, 3), ('wf', 0), ('z', 3, 3), ('z', 0, 2), ('z', 1, 2),
+    ('z', 3, 4), ('z', 2, 4), ('z', 0, 3), ('z', 1, 3), ('z', 4, 1), ('w0', 3),
+    ('zd', 3), ('zd', 2), ('z', 5, 2), ('ids',), ('x1', 1), ('x1', 5),
+    ('q',), ('qw', 0), ('wf', 1), ('z', 1, 4), ('z', 0, 4), ('z', 4, 2),
+    ('z', 7, 1), ('x2', 1), ('zd', 1), ('wf', 2), ('z', 5, 3), ('x2', 5),
+    ('zd', 0), ('z', 4, 3), ('x1', 4), ('qw', 1), ('z', 6, 1), ('z', 7, 2),
+    ('x1', 0), ('qw', 2), ('z', 5, 4), ('x3', 5), ('x2', 4), ('z', 4, 4),
+    ('z', 6, 2), ('x3', 1), ('x2', 0), ('z', 7, 3), ('zd', 5), ('wf', 3),
+    ('zd', 4), ('x1', 6), ('qw', 3), ('z', 6, 3), ('x1', 2), ('x3', 4),
+    ('wr', 1), ('z', 7, 4), ('x2', 6), ('z', 6, 4), ('x3', 0), ('x2', 2),
+    ('zd', 6), ('zd', 7), ('x1', 3), ('x3', 6), ('x1', 7), ('x2', 3),
+    ('x3', 2), ('x2', 7), ('wr', 0), ('x3', 3), ('x3', 7), ('en', 0),
+    ('en', 1), ('en', 2), ('at', 0), ('er', 0, 0), ('er', 0, 1), ('er', 0, 2),
+    ('er', 1, 0), ('er', 1, 1), ('er', 1, 2), ('ef', 0), ('ef', 1), ('er', 2, 0),
+    ('er', 2, 1), ('er', 2, 2), ('at', 5), ('er', 3, 0), ('er', 3, 1), ('er', 3, 2),
+    ('at', 7), ('hb',), ('at', 2), ('at', 3), ('at', 1), ('at', 4),
+    ('at', 6),
 )
 LOG2E = 1.4426950408889634
 BF = jnp.bfloat16
@@ -64,7 +65,7 @@
         idv, ids_s, table, nbp, nbr, wqkv, wout, wcca, enc, qraw, halo, qpad, back_out, back_in,
         normed, ctx, upd, qs, values, qw,
         id_sem, load_sem, z_send, z_recv, x_send, x_recv, a_send, a_recv, a_own,
-        w_send, w_recv, b_send, b_recv, e_send, e_recv, h_send, h_recv,
+        w_send, w_recv, b_send, b_recv, e_send, e_recv, h_send, h_recv, further,
     ) = scratch
 
     seq = lax.axis_index("seq")
@@ -116,13 +117,27 @@
     idv[0] = jnp.zeros((8, 128), jnp.int32)
     idv[0, 0:2, 0:8] = ids_in[...]
 
-    greet = [at(dz=1), at(dz=-1), along(1), along(-1)]
-    greet += [at(dx=dx, dc=dc) for dx in range(NX) for dc in range(NC) if dx or dc]
-    greet += [at(dy=dy, dc=dc) for dy in range(1, NY) for dc in range(NC)]
+    near = [at(dz=1), at(dz=-1), at(dx=1), at(dx=-1), at(dy=1), at(dy=-1), at(dc=1)]
     barrier = pltpu.get_barrier_semaphore()
-    for device in greet:
-        pl.semaphore_signal(barrier, inc=1, device_id=device, device_id_type=pl.DeviceIdType.MESH)
-    pl.semaphore_wait(barrier, len(greet))
+
+    def greet(semaphore):
+        for device in near:
+            pl.semaphore_signal(semaphore, inc=1, device_id=device, device_id_type=pl.DeviceIdType.MESH)
+
+    greet(barrier)
+    pl.semaphore_wait(barrier, len(near))
+
+    def greet_more(step):
+        if step > 0:
+            pl.semaphore_wait(further.at[step - 1], len(near))
+        if step < 2:
+            greet(further.at[step])
+        else:
+            for dx in range(NX):
+                for dc in range(NC):
+                    if dx or dc:
+                        go(id_copy(dx, dc))
+            go(h_query())
 
     def z_copy(f, right, k):
         count = BLOCKS if k < 4 else BLOCKS // 2
@@ -496,13 +511,8 @@
 
     steps = dict(
         z=z_step, zd=z_done, x1=x_step1, x2=x_step2, x3=x_step3, w0=w_start, wf=w_forward, wr=w_rest, q=queries_ready,
-        qw=fold_keys, ids=ids_ready, en=encode_own, er=encode_common, ef=e_forward, at=attend_step, hb=give_back,
+        qw=fold_keys, ids=ids_ready, g=greet_more, en=encode_own, er=encode_common, ef=e_forward, at=attend_step, hb=give_back,
     )
-    for dx in range(NX):
-        for dc in range(NC):
-            if dx or dc:
-                go(id_copy(dx, dc))
-    go(h_query())
     for name, *which in ORDER:
         steps[name](*which)
     h_back().wait_recv()
@@ -548,6 +558,7 @@
         dma((16,)), dma((NF + 4,)), dma((NF, 8)), dma((NF, 8)), dma((NU, 6)), dma((NU, 6)),
         dma((NU, 8)), dma((NU, 8)), dma((NU,)),
         dma((12,)), dma((12,)), dma((12,)), dma((12,)), dma((6,)), dma((6,)), dma((2,)), dma((2,)),
+        pltpu.SemaphoreType.REGULAR((2,)),
     ]
     vmem = pl.BlockSpec(memory_space=pltpu.VMEM)
     hbm = pl.BlockSpec(memory_space=pl.ANY)

time: 108 us -> 107 us (level)
  no operation moved by 1% of the time
where the time goes in v4:
time: 107 us
  Pallas kernels  104 us (97%)
  other arithmetic  2.52 us (2%)
    pallas_call x1, Pallas kernels, fused(): pl.pallas_call(body, out_shape=jax.ShapeDtypeStruct((9, M, D), BF), in_sp...  104 us
    select_n x1, other arithmetic, per_device(): return jnp.where(unserved, jnp.zeros((), BF), attended)  2.52 us

profile of v4, /device:TPU:1, one launch (start us, length us, event | category | flops | bytes accessed | tf_op | source)
XLA Modules:
  0.0 106.8 jit_solution(11755823739346418777)
XLA Ops:
  0.0 104.2 %shard_map.82 = bf16[9,64,1024]{2,1,0:T(8,128)(2,1)} custom-call(s32[2,8]{1,0:T(2,128)} %bitcast.7, bf16[512,1024]{1,0:T(8,128)(2,1)} %queries.1, bf16[16,128,1024]{2,1,0:T(8,128)(2,1)} %database.1, bf16[8,128]{1,0:T(8,128)(2,1)} %bitcast.5, bf16[3,1024,256]{2,1,0:T(8,128)(2,1)} %enc_qkv.1, bf16[256,1024]{1,0:T(8,128)(2,1)} %enc_out.1, ...), custom_call_target="tpu_custom_call" | custom-call | flops 14000000000 | bytes 12582912 | tf_op jit(solution)/shard_map/pallas_call | solution.py:565
  104.2 2.5 %slice_select_fusion = bf16[512,1024]{1,0:T(8,128)(2,1)} fusion(bf16[576,1024]{1,0:T(8,128)(2,1)} %bitcast.4, pred[512]{0:T(512)(128)(4,1)S(1)} %fusion), kind=kLoop, calls=%fused_computation | loop fusion | flops 524288 | bytes 2097664 | tf_op jit(solution)/shard_map/jit(_where)/select_n | solution.py:585
  (1 shorter events, 0.0 us)

commit v5 on v4

--- a/solution.py
+++ b/solution.py
@@ -34,8 +34,8 @@
     ('z', 6, 2), ('x3', 1), ('x2', 0), ('z', 7, 3), ('zd', 5), ('wf', 3),
     ('zd', 4), ('x1', 6), ('qw', 3), ('z', 6, 3), ('x1', 2), ('x3', 4),
     ('wr', 1), ('z', 7, 4), ('x2', 6), ('z', 6, 4), ('x3', 0), ('x2', 2),
-    ('zd', 6), ('zd', 7), ('x1', 3), ('x3', 6), ('x1', 7), ('x2', 3),
-    ('x3', 2), ('x2', 7), ('wr', 0), ('x3', 3), ('x3', 7), ('en', 0),
+    ('zd', 6), ('zd', 7), ('x1', 3), ('x1', 7), ('x3', 6), ('x2', 3),
+    ('x2', 7), ('x3', 2), ('wr', 0), ('x3', 3), ('x3', 7), ('en', 0),
     ('en', 1), ('en', 2), ('at', 0), ('er', 0, 0), ('er', 0, 1), ('er', 0, 2),
     ('er', 1, 0), ('er', 1, 1), ('er', 1, 2), ('ef', 0), ('ef', 1), ('er', 2, 0),
     ('er', 2, 1), ('er', 2, 2), ('at', 5), ('er', 3, 0), ('er', 3, 1), ('er', 3, 2),

time: 107 us -> 107 us (level)
  no operation moved by 1% of the time
where the time goes in v5:
time: 107 us
  Pallas kernels  104 us (97%)
  other arithmetic  2.52 us (2%)
    pallas_call x1, Pallas kernels, fused(): pl.pallas_call(body, out_shape=jax.ShapeDtypeStruct((9, M, D), BF), in_sp...  104 us
    select_n x1, other arithmetic, per_device(): return jnp.where(unserved, jnp.zeros((), BF), attended)  2.52 us

profile of v5, /device:TPU:1, one launch (start us, length us, event | category | flops | bytes accessed | tf_op | source)
XLA Modules:
  0.0 106.7 jit_solution(10588681075099595766)
XLA Ops:
  0.0 104.2 %shard_map.82 = bf16[9,64,1024]{2,1,0:T(8,128)(2,1)} custom-call(s32[2,8]{1,0:T(2,128)} %bitcast.7, bf16[512,1024]{1,0:T(8,128)(2,1)} %queries.1, bf16[16,128,1024]{2,1,0:T(8,128)(2,1)} %database.1, bf16[8,128]{1,0:T(8,128)(2,1)} %bitcast.5, bf16[3,1024,256]{2,1,0:T(8,128)(2,1)} %enc_qkv.1, bf16[256,1024]{1,0:T(8,128)(2,1)} %enc_out.1, ...), custom_call_target="tpu_custom_call" | custom-call | flops 14000000000 | bytes 12582912 | tf_op jit(solution)/shard_map/pallas_call | solution.py:565
  104.2 2.5 %slice_select_fusion = bf16[512,1024]{1,0:T(8,128)(2,1)} fusion(bf16[576,1024]{1,0:T(8,128)(2,1)} %bitcast.4, pred[512]{0:T(512)(128)(4,1)S(1)} %fusion), kind=kLoop, calls=%fused_computation | loop fusion | flops 524288 | bytes 2097664 | tf_op jit(solution)/shard_map/jit(_where)/select_n | solution.py:585
  (1 shorter events, 0.0 us)
